TPU v7x, 128 devices: a whole 4x4x4 slice. The times are simulated.
128 devices in a mesh: dp: 4 (over z_hi, core), blk: 8 (over z_lo, y), ulysses: 4 (over x).
Axes of the slice: x: 4, y: 4, z: 4 (z_hi: 2, z_lo: 2; z = z_hi * 2 + z_lo), core: 2. Of those that a mesh axis runs over, the one named last changes fastest.
Arguments:
- queries: bfloat16 [4, 4096, 2048], P('dp', ('blk', 'ulysses')), may hold values from -8 to 8
- key_vectors: bfloat16 [4, 4096, 512], P('dp', ('blk', 'ulysses')), may hold values from -6 to 6
- value_vectors: bfloat16 [4, 4096, 512], P('dp', ('blk', 'ulysses')), may hold values from -6 to 6
- positions: int32 [4, 4096], P('dp'), may hold values from 0 to 4095, as said below
- out_weight: bfloat16 [2048, 4096], P(('dp', 'blk'), 'ulysses'), may hold values from -0.125 to 0.125
- out_grad: bfloat16 [4, 4096, 4096], P('dp', 'blk', 'ulysses'), may hold values from -6 to 6
Outputs:
- layer_output: bfloat16 [4, 4096, 4096], P('dp', 'blk', 'ulysses')
- query_grad: bfloat16 [4, 4096, 2048], P('dp', ('blk', 'ulysses'))
- key_grad: bfloat16 [4, 4096, 512], P('dp', ('blk', 'ulysses'))
- value_grad: bfloat16 [4, 4096, 512], P('dp', ('blk', 'ulysses'))
- weight_grad: float32 [2048, 4096], P(('dp', 'blk'), 'ulysses')
Inputs may be any that keep to these rules, and one draw needn't show every extreme that they name: Every position of a sequence appears once. Tokens come in runs of 256 that hold consecutive positions, each run starting at a multiple of 256; the tokens of one index of blk are two such runs.
All inputs are finite; a program needn't handle non-finite values.
Results may differ from a plain program's by a relative error of at most 0.035.
Values may be sent and summed in bfloat16 or wider, within the bound.
No kernel may reach another device: no remote copies, remote signals or barrier semaphores. Data moves between devices by JAX's collectives and lax.ppermute only.
A program may use at most 192 MiB of HBM per device.

v0:
```python
import functools
import math

import jax
import jax.numpy as jnp
from jax import lax
from jax.experimental import pallas as pl
from jax.experimental.pallas import tpu as pltpu
from jax.sharding import Mesh
from jax.sharding import PartitionSpec as P

HD = 128
GROUP = 4
SEG = 256
SCALE = HD ** (-0.5)
LOG2_SCALE = SCALE * math.log2(math.e)
MASKED = -1e30
BF16 = jnp.bfloat16
F32 = jnp.float32
VMEM_LIMIT = 48 * 1024 * 1024
SHORT = pl.CostEstimate(flops=1, bytes_accessed=1, transcendentals=0)
PLANE = ("zhi", "zlo", "y")
BLOCK = ("zlo", "y")


def dot(a, b):
    return jnp.dot(a, b, preferred_element_type=F32)


def dot_nt(a, b):
    return lax.dot_general(a, b, (((1,), (1,)), ((), ())), preferred_element_type=F32)


def diagonal_mask():
    key_index = lax.broadcasted_iota(jnp.int32, (SEG, SEG), 0)
    query_index = lax.broadcasted_iota(jnp.int32, (SEG, SEG), 1)
    return key_index <= query_index


def pipeline(units, score, soften, mix):
    now = score(units[0])
    state = None
    for i in range(len(units) + 1):
        following = score(units[i + 1]) if i + 1 < len(units) else None
        if state is not None:
            mix(units[i - 1], state)
        if i < len(units):
            state = soften(units[i], now)
        now = following


def forward_kernel(order_ref, rank_ref, source_ref, *refs):
    pieces, (kv_ref, q_ref, att_t_ref, lse_ref, q_t, v_t, acc, peak, total) = refs[:-9], refs[-9:]
    own = pieces[0].shape[0]
    for i, piece in enumerate(pieces):
        place = pl.multiple_of(source_ref[i] * own, own)
        q_ref[pl.ds(place, own), :] = piece[...]
    runs = q_ref.shape[0] // SEG
    heads = q_ref.shape[1] // HD
    key_runs = kv_ref.shape[0] // SEG

    q_t[...] = q_ref[...].T

    @pl.loop(0, key_runs)
    def _(j):
        rows = pl.ds(pl.multiple_of(j * SEG, SEG), SEG)
        v_t[j] = kv_ref[rows, HD:].T

    for run in range(runs):
        cols = pl.ds(run * SEG, SEG)
        rank = rank_ref[run]

        def tiles(groups, first):
            units = [(g, h) for g in range(len(groups)) for h in range(heads)]
            keys = [
                [kv_ref[pl.ds(pl.multiple_of(j * SEG, SEG), SEG), :HD] for j in group]
                for group in groups
            ]
            values = [[v_t[j] for j in group] for group in groups]

            def score(unit):
                g, h = unit
                queries = q_t[pl.ds(h * HD, HD), cols]
                return [dot(k, queries) for k in keys[g]]

            def soften(unit, scores):
                g, h = unit
                if first and g == 0:
                    mask = diagonal_mask()
                    scores = [jnp.where(mask, s, MASKED) for s in scores]
                top = functools.reduce(
                    jnp.maximum, [jnp.max(s, axis=0, keepdims=True) for s in scores]
                )
                factor = None
                if not (first and g == 0):
                    old = peak[pl.ds(h, 1), :]
                    top = jnp.maximum(top, old)
                    factor = jnp.exp2((old - top) * LOG2_SCALE)
                peak[pl.ds(h, 1), :] = top
                shift = top * LOG2_SCALE
                weights = [jnp.exp2(s * LOG2_SCALE - shift) for s in scores]
                summed = functools.reduce(
                    jnp.add, [jnp.sum(w, axis=0, keepdims=True) for w in weights]
                )
                return factor, summed, [w.astype(BF16) for w in weights]

            def mix(unit, state):
                g, h = unit
                factor, summed, weights = state
                mixed = functools.reduce(
                    jnp.add, [dot(v, w) for v, w in zip(values[g], weights)]
                )
                if factor is None:
                    total[pl.ds(h, 1), :] = summed
                    acc[pl.ds(h * HD, HD), :] = mixed
                else:
                    total[pl.ds(h, 1), :] = total[pl.ds(h, 1), :] * factor + summed
                    acc[pl.ds(h * HD, HD), :] = acc[pl.ds(h * HD, HD), :] * factor + mixed

            pipeline(units, score, soften, mix)

        rest = rank % 4
        for left in range(4):

            @pl.when(rest == left)
            def _():
                groups = [[order_ref[rank]]]
                if left >= 2:
                    groups.append([order_ref[rank - 1], order_ref[rank - 2]])
                if left % 2:
                    groups.append([order_ref[rank - left]])
                tiles(groups, True)

        @pl.loop(0, rank // 4)
        def _(quad):
            start = 4 * quad
            tiles(
                [
                    [order_ref[start], order_ref[start + 1]],
                    [order_ref[start + 2], order_ref[start + 3]],
                ],
                False,
            )

        for h in range(heads):
            row_total = total[pl.ds(h, 1), :]
            lse_ref[pl.ds(h, 1), cols] = peak[pl.ds(h, 1), :] * LOG2_SCALE + jnp.log2(row_total)
            out = (acc[pl.ds(h * HD, HD), :] / row_total).astype(BF16)
            att_t_ref[pl.ds(h * HD, HD), cols] = out


def attend(order, rank, source, pieces, kv):
    own, width = pieces[0].shape
    rows = own * len(pieces)
    heads = width // HD
    length = kv.shape[0]
    smem = pl.BlockSpec(memory_space=pltpu.SMEM)
    vmem = pl.BlockSpec(memory_space=pltpu.VMEM)
    return pl.pallas_call(
        forward_kernel,
        name="attention_forward",
        out_shape=(
            jax.ShapeDtypeStruct((rows, width), BF16),
            jax.ShapeDtypeStruct((width, rows), BF16),
            jax.ShapeDtypeStruct((heads, rows), F32),
        ),
        in_specs=[smem, smem, smem] + [vmem] * (len(pieces) + 1),
        out_specs=(vmem, vmem, vmem),
        scratch_shapes=[
            pltpu.VMEM((width, rows), BF16),
            pltpu.VMEM((length // SEG, HD, SEG), BF16),
            pltpu.VMEM((width, SEG), F32),
            pltpu.VMEM((8, SEG), F32),
            pltpu.VMEM((8, SEG), F32),
        ],
        compiler_params=pltpu.CompilerParams(vmem_limit_bytes=VMEM_LIMIT),
        cost_estimate=pl.CostEstimate(
            flops=4 * rows * length * width,
            bytes_accessed=2 * (3 * rows * width + length * 2 * HD),
            transcendentals=rows * length * heads,
        ),
    )(order, rank, source, *pieces, kv)


def backward_kernel(
    rank_ref,
    key_rank_ref,
    q_ref,
    kv_ref,
    grad_t_ref,
    att_t_ref,
    lse_ref,
    dq_ref,
    dkv_ref,
    q_t,
    grad,
    delta,
    dq_t,
    dk,
    dv,
):
    runs = q_ref.shape[0] // SEG
    heads = q_ref.shape[1] // HD
    key_runs = kv_ref.shape[0] // SEG

    q_t[...] = q_ref[...].T
    grad[...] = grad_t_ref[...].T
    dq_t[...] = jnp.zeros_like(dq_t)
    for h in range(heads):
        part = pl.ds(h * HD, HD)
        delta[pl.ds(h, 1), :] = jnp.sum(
            grad_t_ref[part, :].astype(F32) * att_t_ref[part, :].astype(F32),
            axis=0,
            keepdims=True,
        )

    @pl.loop(0, key_runs)
    def _(j):
        rows = pl.ds(pl.multiple_of(j * SEG, SEG), SEG)
        key_rank = key_rank_ref[j]
        dk[...] = jnp.zeros_like(dk)
        dv[...] = jnp.zeros_like(dv)

        def tile(chosen, masked):
            keys = kv_ref[rows, :HD]
            values = kv_ref[rows, HD:]
            keys_t = keys.T
            sums = [dk[...], dv[...]]
            units = [(run, h) for run in chosen for h in range(heads)]

            def place(unit):
                return pl.ds(unit[1] * HD, HD), pl.ds(unit[0] * SEG, SEG)

            def score(unit):
                part, cols = place(unit)
                return dot(keys, q_t[part, cols]), dot(values, grad_t_ref[part, cols])

            def soften(unit, state):
                scores, prob_grad = state
                _, cols = place(unit)
                row = pl.ds(unit[1], 1)
                probs = jnp.exp2(scores * LOG2_SCALE - lse_ref[row, cols])
                if masked:
                    probs = jnp.where(diagonal_mask(), probs, 0.0)
                score_grad = (probs * (prob_grad - delta[row, cols])).astype(BF16)
                return probs.astype(BF16), score_grad

            def mix(unit, state):
                probs, score_grad = state
                part, cols = place(unit)
                dq_t[part, cols] += dot(keys_t, score_grad)
                sums[0] = sums[0] + dot(score_grad, q_ref[cols, part])
                sums[1] = sums[1] + dot(probs, grad[cols, part])

            pipeline(units, score, soften, mix)
            dk[...] = sums[0]
            dv[...] = sums[1]

        whole = [key_rank < rank_ref[run] for run in range(runs)]
        every = functools.reduce(jnp.logical_and, whole)
        pl.when(every)(functools.partial(tile, range(runs), False))
        for run in range(runs):
            alone = jnp.logical_and(whole[run], jnp.logical_not(every))
            pl.when(alone)(functools.partial(tile, [run], False))
            pl.when(key_rank == rank_ref[run])(functools.partial(tile, [run], True))
        dkv_ref[rows, :HD] = (dk[...] * SCALE).astype(BF16)
        dkv_ref[rows, HD:] = dv[...].astype(BF16)

    for run in range(runs):
        cols = pl.ds(run * SEG, SEG)
        for h in range(heads):
            part = pl.ds(h * HD, HD)
            dq_ref[cols, part] = (dq_t[part, cols] * SCALE).astype(BF16).T


def attend_back(rank, key_rank, q, kv, grad_t, att_t, lse):
    rows, width = q.shape
    heads = width // HD
    length = kv.shape[0]
    smem = pl.BlockSpec(memory_space=pltpu.SMEM)
    vmem = pl.BlockSpec(memory_space=pltpu.VMEM)
    return pl.pallas_call(
        backward_kernel,
        name="attention_backward",
        out_shape=(
            jax.ShapeDtypeStruct((rows, width), BF16),
            jax.ShapeDtypeStruct((length, 2 * HD), BF16),
        ),
        in_specs=[smem, smem] + [vmem] * 5,
        out_specs=(vmem, vmem),
        scratch_shapes=[
            pltpu.VMEM((width, rows), BF16),
            pltpu.VMEM((rows, width), BF16),
            pltpu.VMEM((8, rows), F32),
            pltpu.VMEM((width, rows), F32),
            pltpu.VMEM((SEG, HD), F32),
            pltpu.VMEM((SEG, HD), F32),
        ],
        compiler_params=pltpu.CompilerParams(vmem_limit_bytes=VMEM_LIMIT),
        cost_estimate=pl.CostEstimate(
            flops=10 * rows * length * width,
            bytes_accessed=2 * (4 * rows * width + 2 * length * 2 * HD),
            transcendentals=rows * length * heads,
        ),
    )(rank, key_rank, q, kv, grad_t, att_t, lse)


def pack_kernel(target_ref, q_ref, k_ref, v_ref, kv_ref, *pieces):
    width = pieces[0].shape[1]
    for i, piece in enumerate(pieces):
        columns = pl.ds(pl.multiple_of(target_ref[i] * width, width), width)
        piece[...] = q_ref[0, :, columns]
        kv_ref[i, :, :HD] = k_ref[0, :, pl.ds(i * HD, HD)]
        kv_ref[i, :, HD:] = v_ref[0, :, pl.ds(i * HD, HD)]


def pack(target, queries, key_vectors, value_vectors):
    own = queries.shape[1]
    parts = key_vectors.shape[2] // HD
    width = queries.shape[2] // parts
    smem = pl.BlockSpec(memory_space=pltpu.SMEM)
    vmem = pl.BlockSpec(memory_space=pltpu.VMEM)
    return pl.pallas_call(
        pack_kernel,
        name="pack_heads",
        in_specs=[smem, vmem, vmem, vmem],
        out_specs=(vmem,) * (parts + 1),
        out_shape=(jax.ShapeDtypeStruct((parts, own, 2 * HD), BF16),)
        + (jax.ShapeDtypeStruct((own, width), BF16),) * parts,
    )(target, queries, key_vectors, value_vectors)


def choose(mine, first, second, run):
    pl.when(mine)(functools.partial(run, first))
    pl.when(jnp.logical_not(mine))(functools.partial(run, second))


def fetch_weight(group_ref, core_ref, mine_ref, other_ref, slots, sems):
    for i in range(slots.shape[0]):
        group = group_ref[i]

        def start(weight, i=i, group=group):
            pltpu.make_async_copy(weight.at[group % 2], slots.at[i], sems.at[i]).start()

        choose(group // 2 == core_ref[0], mine_ref, other_ref, start)


def arrived(slots, sems, i):
    pltpu.make_async_copy(slots.at[i], slots.at[i], sems.at[i]).wait()
    return slots[i]


def fetch_columns(sources, slots, sems):
    *pieces, first, second = sources
    half = first.shape[0]
    last = len(pieces)
    copies = [
        pltpu.make_async_copy(piece.at[0], slots.at[i], sems.at[i]) for i, piece in enumerate(pieces)
    ]
    copies.append(pltpu.make_async_copy(first, slots.at[last, pl.ds(0, half)], sems.at[last]))
    copies.append(
        pltpu.make_async_copy(second, slots.at[last, pl.ds(half, half)], sems.at[last + 1])
    )
    for copy in copies:
        copy.start()
    return [[copy] for copy in copies[:last]] + [copies[last:]]


def grad_kernel(group_ref, core_ref, mine_ref, other_ref, *refs):
    *sources, out_ref, total, weights, columns, weight_sems, column_sems = refs
    fetch_weight(group_ref, core_ref, mine_ref, other_ref, weights, weight_sems)
    copies = fetch_columns(sources, columns, column_sems)
    for i, waits in enumerate(copies):
        weight = arrived(weights, weight_sems, i)
        for copy in waits:
            copy.wait()
        term = dot_nt(weight, columns[i])
        total[...] = term if i == 0 else total[...] + term
    out_ref[...] = total[...].astype(BF16)


def project_back(groups, core, mine, other, pieces):
    width, rows = mine.shape[1], pieces[0].shape[1]
    smem = pl.BlockSpec(memory_space=pltpu.SMEM)
    vmem = pl.BlockSpec(memory_space=pltpu.VMEM)
    far = pl.BlockSpec(memory_space=pl.ANY)
    count, columns = groups.shape[0], mine.shape[2]
    return pl.pallas_call(
        grad_kernel,
        name="attention_grad",
        in_specs=[smem, smem] + [far] * (2 + len(pieces)),
        out_specs=vmem,
        out_shape=jax.ShapeDtypeStruct((width, rows), BF16),
        scratch_shapes=[
            pltpu.VMEM((width, rows), F32),
            pltpu.VMEM((count, width, columns), BF16),
            pltpu.VMEM((count, rows, columns), BF16),
            pltpu.SemaphoreType.DMA((count,)),
            pltpu.SemaphoreType.DMA((count + 1,)),
        ],
        compiler_params=pltpu.CompilerParams(vmem_limit_bytes=VMEM_LIMIT),
        cost_estimate=SHORT,
    )(groups, core, mine, other, *pieces)


def weight_grad_kernel(group_ref, core_ref, att_t_ref, *refs):
    *sources, mine_ref, other_ref, columns, column_sems = refs
    copies = fetch_columns(sources, columns, column_sems)
    for i, waits in enumerate(copies):
        group = group_ref[i]
        for copy in waits:
            copy.wait()

        def product(out, i=i, group=group):
            out[group % 2] = dot(att_t_ref[...], columns[i]).astype(BF16)

        choose(group // 2 == core_ref[0], mine_ref, other_ref, product)


def weight_grad_parts(groups, core, att_t, pieces):
    count = groups.shape[0]
    out = jax.ShapeDtypeStruct((count // 2, att_t.shape[0], pieces[0].shape[2]), BF16)
    smem = pl.BlockSpec(memory_space=pltpu.SMEM)
    vmem = pl.BlockSpec(memory_space=pltpu.VMEM)
    far = pl.BlockSpec(memory_space=pl.ANY)
    return pl.pallas_call(
        weight_grad_kernel,
        name="weight_grad_parts",
        in_specs=[smem, smem, vmem] + [far] * len(pieces),
        out_specs=(vmem, vmem),
        out_shape=(out, out),
        scratch_shapes=[
            pltpu.VMEM((count, *pieces[0].shape[1:]), BF16),
            pltpu.SemaphoreType.DMA((count + 1,)),
        ],
        compiler_params=pltpu.CompilerParams(vmem_limit_bytes=VMEM_LIMIT),
        cost_estimate=SHORT,
    )(groups, core, att_t, *pieces)


def output_kernel(group_ref, core_ref, mine_ref, other_ref, att_t_ref, *refs):
    *outs, first, second, att, weights, weight_sems = refs
    half = first.shape[0]
    fetch_weight(group_ref, core_ref, mine_ref, other_ref, weights, weight_sems)
    att[...] = att_t_ref[...].T
    for i, out in enumerate(outs):
        out[...] = dot(att[...], arrived(weights, weight_sems, i)).astype(out.dtype)
    weight = arrived(weights, weight_sems, len(outs))
    first[...] = dot(att[:half, :], weight).astype(BF16)
    second[...] = dot(att[half:, :], weight).astype(BF16)


def project(groups, core, mine, other, att_t):
    count = groups.shape[0]
    width, rows = att_t.shape
    columns = mine.shape[2]
    smem = pl.BlockSpec(memory_space=pltpu.SMEM)
    vmem = pl.BlockSpec(memory_space=pltpu.VMEM)
    far = pl.BlockSpec(memory_space=pl.ANY)
    return pl.pallas_call(
        output_kernel,
        name="layer_output_parts",
        in_specs=[smem, smem, far, far, vmem],
        out_specs=(vmem,) * (count + 1),
        out_shape=(
            jax.ShapeDtypeStruct((rows, columns), F32),
            jax.ShapeDtypeStruct((rows, columns), BF16),
            jax.ShapeDtypeStruct((rows, columns), BF16),
            jax.ShapeDtypeStruct((rows // 2, columns), BF16),
            jax.ShapeDtypeStruct((rows // 2, columns), BF16),
        ),
        scratch_shapes=[
            pltpu.VMEM((rows, width), BF16),
            pltpu.VMEM((count, width, columns), BF16),
            pltpu.SemaphoreType.DMA((count,)),
        ],
        compiler_params=pltpu.CompilerParams(vmem_limit_bytes=VMEM_LIMIT),
        cost_estimate=SHORT,
    )(groups, core, mine, other, att_t)


def finish_kernel(source_ref, *refs):
    pieces, dkv_ref, (dq_ref, dk_ref, dv_ref) = refs[:-4], refs[-4], refs[-3:]
    width = pieces[0].shape[1]
    for i, piece in enumerate(pieces):
        columns = pl.ds(pl.multiple_of(source_ref[i] * width, width), width)
        dq_ref[0, :, columns] = piece[...]
    blocks, parts = dkv_ref.shape[:2]
    for u in range(parts):
        total = dkv_ref[0, u].astype(F32)
        for b in range(1, blocks):
            total = total + dkv_ref[b, u].astype(F32)
        total = total.astype(BF16)
        dk_ref[0, :, pl.ds(u * HD, HD)] = total[:, :HD]
        dv_ref[0, :, pl.ds(u * HD, HD)] = total[:, HD:]


def finish(source, pieces, dkv):
    own, width = pieces[0].shape
    parts = len(pieces)
    smem = pl.BlockSpec(memory_space=pltpu.SMEM)
    vmem = pl.BlockSpec(memory_space=pltpu.VMEM)
    return pl.pallas_call(
        finish_kernel,
        name="gather_gradients",
        in_specs=[smem] + [vmem] * (parts + 1),
        out_specs=(vmem, vmem, vmem),
        out_shape=(
            jax.ShapeDtypeStruct((1, own, parts * width), BF16),
            jax.ShapeDtypeStruct((1, own, parts * HD), BF16),
            jax.ShapeDtypeStruct((1, own, parts * HD), BF16),
        ),
        compiler_params=pltpu.CompilerParams(vmem_limit_bytes=VMEM_LIMIT),
    )(source, *pieces, dkv)


def exchange(array, axes):
    return lax.all_to_all(array, axes, split_axis=0, concat_axis=0, tiled=True)


def shift(array, axis, by):
    length = lax.axis_size(axis)
    return lax.ppermute(array, axis, [(i, (i + by) % length) for i in range(length)])


def pick(array, index):
    return lax.dynamic_index_in_dim(array, index, 0, keepdims=False)


def put(array, piece, index):
    return lax.dynamic_update_index_in_dim(array, piece, index, 0)


def spread(array, count):
    return jnp.broadcast_to(array[None], (count,) + array.shape).reshape(
        (count * array.shape[0],) + array.shape[1:]
    )


def swap_pairs():
    pairs = []
    for zhi in range(2):
        for core in range(2):
            for x in range(4):
                source = (zhi * 2 + core) * 4 + x
                target = ((x % 2) * 2 + x // 2) * 4 + zhi * 2 + core
                pairs.append((source, target))
    return pairs


def swap(array):
    return lax.ppermute(array, ("zhi", "core", "x"), swap_pairs())


def swap_back(array):
    return lax.ppermute(array, ("zhi", "core", "x"), [(b, a) for a, b in swap_pairs()])


def flip(array, by):
    return lax.ppermute(array, "x", [(i, i ^ by) for i in range(4)])


def after(array, *others):
    return lax.optimization_barrier((array,) + others)[0]


def shards(queries, key_vectors, value_vectors, positions, out_weight, out_grad):
    x = lax.axis_index("x")
    core = lax.axis_index("core")
    blk = lax.axis_index(BLOCK)
    xs = lax.axis_size("x")
    own = queries.shape[1]
    width = queries.shape[2] // xs
    blocks = lax.axis_size(BLOCK)
    rows = own * xs
    columns = out_grad.shape[2]

    key_rank = positions[0, ::SEG] // SEG
    count = key_rank.shape[0]
    index = jnp.arange(count, dtype=jnp.int32)
    order = jnp.sum(
        jnp.where(key_rank[None, :] == index[:, None], index[None, :], 0), axis=1
    ).astype(jnp.int32)
    rank = lax.dynamic_slice_in_dim(key_rank, blk * (rows // SEG), rows // SEG)

    steps = jnp.arange(xs, dtype=jnp.int32)
    target, source = (x + steps) % xs, (x - steps) % xs

    weight_swapped = swap(out_weight)
    kv_parts, *q_parts = pack(target, queries, key_vectors, value_vectors)
    q_pieces = q_parts[:1] + [shift(q_parts[d], "x", d) for d in range(1, xs)]
    kv = exchange(spread(kv_parts, blocks), BLOCK + ("x",)).reshape(blocks * rows, 2 * HD)

    near = jnp.stack([x, x ^ 1, x ^ 3, x ^ 2]).astype(jnp.int32)
    half = rows // 2
    og_own = after(out_grad, kv, weight_swapped, *q_pieces)
    og_1, og_3 = flip(og_own, 1), flip(og_own, 3)

    weight_swapped = after(weight_swapped, kv, *q_pieces)
    weight_half = exchange(spread(weight_swapped, 2 * blocks), PLANE)

    q, att_t, lse = attend(order, rank, source, q_pieces, kv)

    og_1, og_3, _ = lax.optimization_barrier((og_1, og_3, att_t))
    og = [out_grad, og_1, og_3, flip(og_1[0, :half], 3), flip(og_3[0, half:], 1)]

    weight_mine = after(weight_half, att_t).reshape(2, width, columns)
    weight_other = shift(weight_mine, "core", 1)

    cores = core.astype(jnp.int32).reshape(1)
    wg_mine, wg_sent = weight_grad_parts(near, cores, att_t, og)
    grad_t = project_back(near, cores, weight_mine, weight_other, og)

    wg_got = after(shift(wg_sent, "core", 1), grad_t)
    wg_half = (wg_mine.astype(F32) + wg_got.astype(F32)).astype(BF16)
    wg_half = wg_half.reshape(2 * blocks, width // blocks, columns)
    wg_parts = exchange(wg_half, PLANE)
    weight_grad = swap_back(jnp.sum(wg_parts.astype(F32), axis=0))

    lo, lo_1, lo_3, lo_first, lo_second = project(near, cores, weight_mine, weight_other, att_t)
    lo_3 = lo_3.at[:half].add(flip(lo_first, 1))
    lo_1 = lo_1.at[half:].add(flip(lo_second, 3))
    lo = lo + flip(lo_1, 1).astype(F32) + flip(lo_3, 3).astype(F32)
    layer_output = lo.astype(BF16)[None]

    grad_t = after(grad_t, wg_half, lo_1, lo_3)
    dq, dkv = attend_back(rank, key_rank, q, kv, grad_t, att_t, lse)

    dkv = after(dkv, layer_output)
    dq_parts = dq.reshape(xs, own, width)
    pieces = [pick(dq_parts, x)]
    for d in range(1, xs):
        pieces.append(shift(pick(dq_parts, (x + d) % xs), "x", d))
    dkv_got = exchange(dkv.reshape(blocks * xs, own, 2 * HD), BLOCK + ("x",))
    dkv_got = dkv_got.reshape(blocks, xs, own, 2 * HD)
    query_grad, key_grad, value_grad = finish(source, pieces, dkv_got)
    return (layer_output, query_grad, key_grad, value_grad, weight_grad)


def solution(mesh):
    split = Mesh(mesh.devices.reshape(2, 2, 2, 4, 4), ("zhi", "core", "zlo", "y", "x"))
    dp = ("zhi", "core")
    tokens = P(dp, ("zlo", "y", "x"), None)
    weight = P(("zhi", "core", "zlo", "y"), "x")
    columns = P(dp, BLOCK, "x")
    return jax.shard_map(
        shards,
        mesh=split,
        in_specs=(tokens, tokens, tokens, P(dp, None), weight, columns),
        out_specs=(columns, tokens, tokens, tokens, weight),
        check_vma=False,
    )
```

profile of v0, /device:TPU:0, one launch (start us, length us, event | category | flops | bytes accessed | tf_op | source)
XLA Modules:
  0.0 204.5 jit_solution(2453049648632764241)
XLA Ops:
  1.2 2.1 %pack_heads.1 = (bf16[4,128,256]{2,1,0:T(8,128)(2,1)}, bf16[128,512]{1,0:T(8,128)(2,1)}, bf16[128,512]{1,0:T(8,128)(2,1)}, bf16[128,512]{1,0:T(8,128)(2,1)}, bf16[128,512]{1,0:T(8,128)(2,1)}) custom-call(s32[4]{0:T(128)} %and_select_fusion.3.target_ref, bf16[1,128,2048]{2,1,0:T(8,128)(2,1)} %q_ref.1, bf16[1,128,512]{2,1,0:T(8,128)(2,1)} %k_ref.1, ...), custom_call_target="tpu_custom_call" | custom-call | tf_op jit(solution)/shard_map/pack_heads/pallas_call | solution.py:323
  3.3 2.5 %broadcast_in_dim.18 = bf16[8,4,128,256]{3,2,1,0:T(8,128)(2,1)} broadcast(bf16[4,128,256]{2,1,0:T(8,128)(2,1)} %get-tuple-element.57), dimensions={1,2,3} | broadcast | bytes 2359296 | tf_op jit(solution)/shard_map/broadcast_in_dim | solution.py:535
  5.8 8.9 %all-to-all-start = ((bf16[32,128,256]{2,1,0:T(8,128)(2,1)}), bf16[32,128,256]{2,1,0:T(8,128)(2,1)S(1)}, u32[]{:S(2)}, u32[]{:S(2)}) async-start(bf16[32,128,256]{2,1,0:T(8,128)(2,1)} %bitcast.43), calls=%async_computation | async-start | bytes 4194304 | tf_op jit(solution)/shard_map/all_to_all | solution.py:518
  14.7 1.9 collective-permute-start.1
  16.6 2.7 %collective-permute-start.2 = (bf16[128,512]{1,0:T(8,128)(2,1)}, bf16[128,512]{1,0:T(8,128)(2,1)S(1)}, u32[]{:S(2)}, u32[]{:S(2)}) collective-permute-start(bf16[128,512]{1,0:T(8,128)(2,1)} %get-tuple-element.60), channel_id=1, source_target_pairs={{0,2},{1,3},{2,0},{3,1},{4,6},{5,7},{6,4},{7,5},{8,10},{9,11},{10,... | collective-permute-start | bytes 393224 | tf_op jit(solution)/shard_map/ppermute | solution.py:523
  19.2 1.5 collective-permute-start.3
  20.7 2.1 %collective-permute-start = (bf16[64,1024]{1,0:T(8,128)(2,1)}, bf16[64,1024]{1,0:T(8,128)(2,1)}, u32[]{:S(2)}, u32[]{:S(2)}) collective-permute-start(bf16[64,1024]{1,0:T(8,128)(2,1)} %param.14), channel_id=1, source_target_pairs={{0,0},{1,64},{2,32},{3,96},{32,1},{33,65},{34,33},{35,97},{64,2},{... | collective-permute-start | bytes 393224 | tf_op jit(solution)/shard_map/ppermute | solution.py:552
  23.7 20.5 %collective-permute-done.1.refs_1_ = bf16[128,512]{1,0:T(8,128)(2,1)S(1)} collective-permute-done((bf16[128,512]{1,0:T(8,128)(2,1)}, bf16[128,512]{1,0:T(8,128)(2,1)S(1)}, u32[]{:S(2)}, u32[]{:S(2)}) %collective-permute-start.1) | collective-permute-done | bytes 131104 | tf_op jit(solution)/shard_map/ppermute | solution.py:523
  44.1 2.5 %collective-permute-done.2.refs_2_ = bf16[128,512]{1,0:T(8,128)(2,1)S(1)} collective-permute-done((bf16[128,512]{1,0:T(8,128)(2,1)}, bf16[128,512]{1,0:T(8,128)(2,1)S(1)}, u32[]{:S(2)}, u32[]{:S(2)}) %collective-permute-start.2) | collective-permute-done | bytes 131104 | tf_op jit(solution)/shard_map/ppermute | solution.py:523
  47.3 1.3 copy-done.4
  48.6 5.0 %collective-permute-start.10 = (bf16[1,512,1024]{2,1,0:T(8,128)(2,1)S(1)}, bf16[1,512,1024]{2,1,0:T(8,128)(2,1)S(1)}, u32[]{:S(2)}, u32[]{:S(2)}) collective-permute-start(bf16[1,512,1024]{2,1,0:T(8,128)(2,1)S(1)} %copy-done), channel_id=1, source_target_pairs={{0,3},{1,2},{2,1},{3,0},{4,7},{5,6},{6,5},{7,4},{8,11},{9,10},{10,... | collective-permute-start | bytes 3145736 | tf_op jit(solution)/shard_map/ppermute | solution.py:560
  53.7 2.5 %broadcast_in_dim.19 = bf16[16,64,1024]{2,1,0:T(8,128)(2,1)} broadcast(bf16[64,1024]{1,0:T(8,128)(2,1)} %collective-permute-done), dimensions={1,2} | broadcast | bytes 2228224 | tf_op jit(solution)/shard_map/broadcast_in_dim | solution.py:535
  56.2 5.3 %all-to-all-start.1 = ((bf16[16,64,1024]{2,1,0:T(8,128)(2,1)}), bf16[16,64,1024]{2,1,0:T(8,128)(2,1)}, u32[]{:S(2)}, u32[]{:S(2)}) async-start(bf16[16,64,1024]{2,1,0:T(8,128)(2,1)} %broadcast_in_dim.19), calls=%async_computation.1 | async-start | bytes 4194304 | tf_op jit(solution)/shard_map/all_to_all | solution.py:518
  61.8 1.6 copy-done.5
  63.4 0.9 copy-done.17
  64.3 8.7 %attention_forward.1 = (bf16[512,512]{1,0:T(8,128)(2,1)S(1)}, bf16[512,512]{1,0:T(8,128)(2,1)S(1)}, f32[4,512]{1,0:T(4,128)S(1)}) custom-call(s32[16]{0:T(128)S(1)} %select_reduce_fusion.order_ref, s32[2]{0:T(128)S(1)} %dynamic_slice.16.rank_ref, s32[4]{0:T(128)S(1)} %and_select_fusion.source_ref, bf16[128,512]{1,0:T(8,128)(2,1)S(1)} %copy-done.15, ...), custom_call_target="tpu_custom_call" | custom-call | flops 4294967296 | bytes 3670016 | tf_op jit(solution)/shard_map/attention_forward/pallas_call | solution.py:159
  75.2 1.2 collective-permute-done.10.refs_2_
  76.3 1.5 collective-permute-done.9.refs_1_
  77.8 0.8 slice_bitcast_fusion.1
  78.6 1.5 collective-permute-start.11
  80.1 0.8 slice_bitcast_fusion
  80.9 10.1 %all-to-all-done.1 = bf16[16,64,1024]{2,1,0:T(8,128)(2,1)} async-done(((bf16[16,64,1024]{2,1,0:T(8,128)(2,1)}), bf16[16,64,1024]{2,1,0:T(8,128)(2,1)}, u32[]{:S(2)}, u32[]{:S(2)}) %all-to-all-start.1) | async-done | bytes 2097184 | tf_op jit(solution)/shard_map/all_to_all | solution.py:518
  91.1 1.1 collective-permute-done.11.refs_3_
  92.2 1.1 collective-permute-done.12.refs_4_
  93.3 1.0 copy-done.2
  94.4 5.8 %weight_grad_parts.1 = (bf16[2,512,1024]{2,1,0:T(8,128)(2,1)}, bf16[2,512,1024]{2,1,0:T(8,128)(2,1)}) custom-call(s32[4]{0:T(128)S(1)} %pad_add_fusion.group_ref, s32[1]{0:T(128)} %bitcast.4.core_ref, bf16[512,512]{1,0:T(8,128)(2,1)S(1)} %copy-done.2, bf16[1,512,1024]{2,1,0:T(8,128)(2,1)S(1)} %copy-done, ...), custom_call_target="tpu_custom_call" | custom-call | flops 1 | bytes 1 | tf_op jit(solution)/shard_map/weight_grad_parts/pallas_call | solution.py:426
  100.2 1.4 copy-done.22
  101.6 5.5 %layer_output_parts.1 = (f32[512,1024]{1,0:T(8,128)S(1)}, bf16[512,1024]{1,0:T(8,128)(2,1)S(1)}, bf16[512,1024]{1,0:T(8,128)(2,1)S(1)}, bf16[256,1024]{1,0:T(8,128)(2,1)}, bf16[256,1024]{1,0:T(8,128)(2,1)}) custom-call(s32[4]{0:T(128)S(1)} %pad_add_fusion.group_ref, s32[1]{0:T(128)} %bitcast.4.core_ref, bf16[2,512,1024]{2,1,0:T(8,128)(2,1)} %bitcast.10.mine_ref, ...), custom_call_target="tpu_custom_call" | custom-call | flops 1 | bytes 1 | tf_op jit(solution)/shard_map/layer_output_parts/pallas_call | solution.py:460
  107.2 1.3 copy-done.7
  108.5 2.4 %collective-permute-start.5 = (bf16[256,1024]{1,0:T(8,128)(2,1)}, bf16[256,1024]{1,0:T(8,128)(2,1)}, u32[]{:S(2)}, u32[]{:S(2)}) collective-permute-start(bf16[256,1024]{1,0:T(8,128)(2,1)} %get-tuple-element.67), channel_id=1, source_target_pairs={{0,3},{1,2},{2,1},{3,0},{4,7},{5,6},{6,5},{7,4},{8,11},{9,10},{10,... | collective-permute-start | bytes 1572872 | tf_op jit(solution)/shard_map/ppermute | solution.py:560
  110.9 4.8 %attention_grad.1.grad_t_ref = bf16[512,512]{1,0:T(8,128)(2,1)S(1)} custom-call(s32[4]{0:T(128)S(1)} %pad_add_fusion.group_ref, s32[1]{0:T(128)} %bitcast.4.core_ref, bf16[2,512,1024]{2,1,0:T(8,128)(2,1)} %bitcast.10.mine_ref, bf16[2,512,1024]{2,1,0:T(8,128)(2,1)} %copy-done.22, bf16[1,512,1024]{2,1,0:T(8,128)(2,1)S(1)} %copy-done, ...), custom_call_target="tpu_custom_call" | custom-call | flops 1 | bytes 1 | tf_op jit(solution)/shard_map/attention_grad/pallas_call | solution.py:388
  116.4 2.4 %add_convert_fusion = bf16[2,512,1024]{2,1,0:T(8,128)(2,1)} fusion(bf16[2,512,1024]{2,1,0:T(8,128)(2,1)S(1)} %collective-permute-done.13, bf16[2,512,1024]{2,1,0:T(8,128)(2,1)S(1)} %copy-done.23), kind=kLoop, calls=%fused_computation.1 | loop fusion | flops 4194304 | bytes 6291456 | tf_op jit(solution)/shard_map/convert_element_type | solution.py:615
  118.8 9.7 %all-to-all-start.3 = ((bf16[16,64,1024]{2,1,0:T(8,128)(2,1)}), bf16[16,64,1024]{2,1,0:T(8,128)(2,1)}, u32[]{:S(2)}, u32[]{:S(2)}) async-start(bf16[16,64,1024]{2,1,0:T(8,128)(2,1)} %bitcast.42), calls=%async_computation.3 | async-start | bytes 4194304 | tf_op jit(solution)/shard_map/all_to_all | solution.py:518
  128.5 1.4 add_dynamic-update-slice_fusion.1
  129.9 1.0 collective-permute-start.6
  131.1 2.5 %collective-permute-start.8 = (bf16[512,1024]{1,0:T(8,128)(2,1)S(1)}, bf16[512,1024]{1,0:T(8,128)(2,1)S(1)}, u32[]{:S(2)}, u32[]{:S(2)}) collective-permute-start(bf16[512,1024]{1,0:T(8,128)(2,1)S(1)} %add_dynamic-update-slice_fusion), channel_id=1, source_target_pairs={{0,3},{1,2},{2,1},{3,0},{4,7},{5,6},{6,5},{7,4},{8,11},{9,10},{10,... | collective-permute-start | bytes 3145736 | tf_op jit(solution)/shard_map/ppermute | solution.py:560
  133.6 13.4 %attention_backward.1 = (bf16[512,512]{1,0:T(8,128)(2,1)S(1)}, bf16[4096,256]{1,0:T(8,128)(2,1)S(1)}) custom-call(s32[2]{0:T(128)S(1)} %dynamic_slice.16.rank_ref, s32[16]{0:T(128)S(1)} %and_select_fusion.1.key_rank_ref, bf16[512,512]{1,0:T(8,128)(2,1)S(1)} %copy-done.19, bf16[4096,256]{1,0:T(8,128)(2,1)} %bitcast.38, bf16[512,512]{1,0:T(8,128)(2,1)S(1)} %copy-done.10, ...), custom_call_target="tpu_custom_call" | custom-call | flops 10737418240 | bytes 6291456 | tf_op jit(solution)/shard_map/attention_backward/pallas_call | solution.py:282
  147.0 7.9 %collective-permute-done.6 = bf16[512,1024]{1,0:T(8,128)(2,1)S(1)} collective-permute-done((bf16[512,1024]{1,0:T(8,128)(2,1)S(1)}, bf16[512,1024]{1,0:T(8,128)(2,1)S(1)}, u32[]{:S(2)}, u32[]{:S(2)}) %collective-permute-start.6) | collective-permute-done | bytes 1048608 | tf_op jit(solution)/shard_map/ppermute | solution.py:560
  155.0 2.1 %collective-permute-done.8 = bf16[512,1024]{1,0:T(8,128)(2,1)S(1)} collective-permute-done((bf16[512,1024]{1,0:T(8,128)(2,1)S(1)}, bf16[512,1024]{1,0:T(8,128)(2,1)S(1)}, u32[]{:S(2)}, u32[]{:S(2)}) %collective-permute-start.8) | collective-permute-done | bytes 1048608 | tf_op jit(solution)/shard_map/ppermute | solution.py:560
  157.1 1.5 fusion
  158.6 3.2 %all-to-all-done.3 = bf16[16,64,1024]{2,1,0:T(8,128)(2,1)} async-done(((bf16[16,64,1024]{2,1,0:T(8,128)(2,1)}), bf16[16,64,1024]{2,1,0:T(8,128)(2,1)}, u32[]{:S(2)}, u32[]{:S(2)}) %all-to-all-start.3) | async-done | bytes 2097184 | tf_op jit(solution)/shard_map/all_to_all | solution.py:518
  161.8 4.0 %all-to-all-start.2 = ((bf16[32,128,256]{2,1,0:T(8,128)(2,1)}), bf16[32,128,256]{2,1,0:T(8,128)(2,1)S(1)}, u32[]{:S(2)}, u32[]{:S(2)}) async-start(bf16[32,128,256]{2,1,0:T(8,128)(2,1)} %bitcast.40), calls=%async_computation.2 | async-start | bytes 4194304 | tf_op jit(solution)/shard_map/all_to_all | solution.py:518
  165.8 2.0 convert_reduce_fusion
  168.6 3.1 %collective-permute-start.14 = (bf16[128,512]{1,0:T(8,128)(2,1)S(1)}, bf16[128,512]{1,0:T(8,128)(2,1)S(1)}, u32[]{:S(2)}, u32[]{:S(2)}) collective-permute-start(bf16[128,512]{1,0:T(8,128)(2,1)S(1)} %get-tuple-element.87), channel_id=1, source_target_pairs={{0,1},{1,2},{2,3},{3,0},{4,5},{5,6},{6,7},{7,4},{8,9},{9,10},{10,1... | collective-permute-start | bytes 393224 | tf_op jit(solution)/shard_map/ppermute | solution.py:523
  171.7 4.7 %collective-permute-start.15 = (bf16[128,512]{1,0:T(8,128)(2,1)S(1)}, bf16[128,512]{1,0:T(8,128)(2,1)S(1)}, u32[]{:S(2)}, u32[]{:S(2)}) collective-permute-start(bf16[128,512]{1,0:T(8,128)(2,1)S(1)} %get-tuple-element.86), channel_id=1, source_target_pairs={{0,2},{1,3},{2,0},{3,1},{4,6},{5,7},{6,4},{7,5},{8,10},{9,11},{10,... | collective-permute-start | bytes 393224 | tf_op jit(solution)/shard_map/ppermute | solution.py:523
  176.4 2.5 %collective-permute-start.16 = (bf16[128,512]{1,0:T(8,128)(2,1)S(1)}, bf16[128,512]{1,0:T(8,128)(2,1)S(1)}, u32[]{:S(2)}, u32[]{:S(2)}) collective-permute-start(bf16[128,512]{1,0:T(8,128)(2,1)S(1)} %get-tuple-element.85), channel_id=1, source_target_pairs={{0,3},{1,0},{2,1},{3,2},{4,7},{5,4},{6,5},{7,6},{8,11},{9,8},{10,9... | collective-permute-start | bytes 393224 | tf_op jit(solution)/shard_map/ppermute | solution.py:523
  179.0 23.2 %collective-permute-done.14.refs_1_ = bf16[128,512]{1,0:T(8,128)(2,1)S(1)} collective-permute-done((bf16[128,512]{1,0:T(8,128)(2,1)S(1)}, bf16[128,512]{1,0:T(8,128)(2,1)S(1)}, u32[]{:S(2)}, u32[]{:S(2)}) %collective-permute-start.14) | collective-permute-done | bytes 131104 | tf_op jit(solution)/shard_map/ppermute | solution.py:523
  202.2 1.6 gather_gradients.1
  (70 shorter events, 7.0 us)
Async XLA Ops:
  5.8 42.8 %copy-start = (bf16[1,512,1024]{2,1,0:T(8,128)(2,1)S(1)}, bf16[1,512,1024]{2,1,0:T(8,128)(2,1)}, u32[]{:S(2)}) copy-start(bf16[1,512,1024]{2,1,0:T(8,128)(2,1)} %refs_0_.3) | copy-start | bytes 3145732
  5.8 41.5 %all-to-all-start = ((bf16[32,128,256]{2,1,0:T(8,128)(2,1)}), bf16[32,128,256]{2,1,0:T(8,128)(2,1)S(1)}, u32[]{:S(2)}, u32[]{:S(2)}) async-start(bf16[32,128,256]{2,1,0:T(8,128)(2,1)} %bitcast.43), calls=%async_computation | async-start | bytes 4194304 | tf_op jit(solution)/shard_map/all_to_all | solution.py:518
  14.7 29.4 %collective-permute-start.1 = (bf16[128,512]{1,0:T(8,128)(2,1)}, bf16[128,512]{1,0:T(8,128)(2,1)S(1)}, u32[]{:S(2)}, u32[]{:S(2)}) collective-permute-start(bf16[128,512]{1,0:T(8,128)(2,1)} %get-tuple-element.59), channel_id=1, source_target_pairs={{0,1},{1,2},{2,3},{3,0},{4,5},{5,6},{6,7},{7,4},{8,9},{9,10},{10,1... | collective-permute-start | bytes 393224 | tf_op jit(solution)/shard_map/ppermute | solution.py:523
  16.6 30.1 %collective-permute-start.2 = (bf16[128,512]{1,0:T(8,128)(2,1)}, bf16[128,512]{1,0:T(8,128)(2,1)S(1)}, u32[]{:S(2)}, u32[]{:S(2)}) collective-permute-start(bf16[128,512]{1,0:T(8,128)(2,1)} %get-tuple-element.60), channel_id=1, source_target_pairs={{0,2},{1,3},{2,0},{3,1},{4,6},{5,7},{6,4},{7,5},{8,10},{9,11},{10,... | collective-permute-start | bytes 393224 | tf_op jit(solution)/shard_map/ppermute | solution.py:523
  19.2 27.4 %collective-permute-start.3 = (bf16[128,512]{1,0:T(8,128)(2,1)}, bf16[128,512]{1,0:T(8,128)(2,1)S(1)}, u32[]{:S(2)}, u32[]{:S(2)}) collective-permute-start(bf16[128,512]{1,0:T(8,128)(2,1)} %get-tuple-element.61), channel_id=1, source_target_pairs={{0,3},{1,0},{2,1},{3,2},{4,7},{5,4},{6,5},{7,6},{8,11},{9,8},{10,9... | collective-permute-start | bytes 393224 | tf_op jit(solution)/shard_map/ppermute | solution.py:523
  20.7 26.6 %collective-permute-start = (bf16[64,1024]{1,0:T(8,128)(2,1)}, bf16[64,1024]{1,0:T(8,128)(2,1)}, u32[]{:S(2)}, u32[]{:S(2)}) collective-permute-start(bf16[64,1024]{1,0:T(8,128)(2,1)} %param.14), channel_id=1, source_target_pairs={{0,0},{1,64},{2,32},{3,96},{32,1},{33,65},{34,33},{35,97},{64,2},{... | collective-permute-start | bytes 393224 | tf_op jit(solution)/shard_map/ppermute | solution.py:552
  46.6 0.7 copy-start.16
  47.3 1.3 copy-start.4
  48.6 27.7 %collective-permute-start.10 = (bf16[1,512,1024]{2,1,0:T(8,128)(2,1)S(1)}, bf16[1,512,1024]{2,1,0:T(8,128)(2,1)S(1)}, u32[]{:S(2)}, u32[]{:S(2)}) collective-permute-start(bf16[1,512,1024]{2,1,0:T(8,128)(2,1)S(1)} %copy-done), channel_id=1, source_target_pairs={{0,3},{1,2},{2,1},{3,0},{4,7},{5,6},{6,5},{7,4},{8,11},{9,10},{10,... | collective-permute-start | bytes 3145736 | tf_op jit(solution)/shard_map/ppermute | solution.py:560
  53.7 24.1 %collective-permute-start.9 = (bf16[1,512,1024]{2,1,0:T(8,128)(2,1)S(1)}, bf16[1,512,1024]{2,1,0:T(8,128)(2,1)S(1)}, u32[]{:S(2)}, u32[]{:S(2)}) collective-permute-start(bf16[1,512,1024]{2,1,0:T(8,128)(2,1)S(1)} %copy-done), channel_id=1, source_target_pairs={{0,1},{1,0},{2,3},{3,2},{4,5},{5,4},{6,7},{7,6},{8,9},{9,8},{10,11... | collective-permute-start | bytes 3145736 | tf_op jit(solution)/shard_map/ppermute | solution.py:560
  56.2 5.6 %copy-start.15 = (bf16[128,512]{1,0:T(8,128)(2,1)S(1)}, bf16[128,512]{1,0:T(8,128)(2,1)}, u32[]{:S(2)}) copy-start(bf16[128,512]{1,0:T(8,128)(2,1)} %get-tuple-element.58.refs_0_) | copy-start | bytes 393220
  56.2 34.8 %all-to-all-start.1 = ((bf16[16,64,1024]{2,1,0:T(8,128)(2,1)}), bf16[16,64,1024]{2,1,0:T(8,128)(2,1)}, u32[]{:S(2)}, u32[]{:S(2)}) async-start(bf16[16,64,1024]{2,1,0:T(8,128)(2,1)} %broadcast_in_dim.19), calls=%async_computation.1 | async-start | bytes 4194304 | tf_op jit(solution)/shard_map/all_to_all | solution.py:518
  61.8 1.6 copy-start.5
  63.4 0.9 copy-start.17
  73.0 0.8 copy-start.1
  73.8 0.8 copy-start.18
  74.6 0.6 copy-start.20
  78.6 13.6 %collective-permute-start.11 = (bf16[256,1024]{1,0:T(8,128)(2,1)}, bf16[256,1024]{1,0:T(8,128)(2,1)}, u32[]{:S(2)}, u32[]{:S(2)}) collective-permute-start(bf16[256,1024]{1,0:T(8,128)(2,1)} %slice_bitcast_fusion.1), channel_id=1, source_target_pairs={{0,3},{1,2},{2,1},{3,0},{4,7},{5,6},{6,5},{7,4},{8,11},{9,10},{10,... | collective-permute-start | bytes 1572872 | tf_op jit(solution)/shard_map/ppermute | solution.py:560
  80.9 12.4 %collective-permute-start.12 = (bf16[256,1024]{1,0:T(8,128)(2,1)}, bf16[256,1024]{1,0:T(8,128)(2,1)}, u32[]{:S(2)}, u32[]{:S(2)}) collective-permute-start(bf16[256,1024]{1,0:T(8,128)(2,1)} %slice_bitcast_fusion), channel_id=1, source_target_pairs={{0,1},{1,0},{2,3},{3,2},{4,5},{5,4},{6,7},{7,6},{8,9},{9,8},{10,11... | collective-permute-start | bytes 1572872 | tf_op jit(solution)/shard_map/ppermute | solution.py:560
  91.0 9.2 %collective-permute-start.4 = (bf16[2,512,1024]{2,1,0:T(8,128)(2,1)}, bf16[2,512,1024]{2,1,0:T(8,128)(2,1)S(1)}, u32[]{:S(2)}, u32[]{:S(2)}) collective-permute-start(bf16[2,512,1024]{2,1,0:T(8,128)(2,1)} %bitcast.10.mine_ref), channel_id=1, source_target_pairs={{0,32},{32,0},{1,33},{33,1},{2,34},{34,2},{3,35},{35,3},{4,36},{36... | collective-permute-start | bytes 6291464 | tf_op jit(solution)/shard_map/ppermute | solution.py:523
  93.3 1.0 copy-start.2
  100.1 15.5 %collective-permute-start.13 = (bf16[2,512,1024]{2,1,0:T(8,128)(2,1)}, bf16[2,512,1024]{2,1,0:T(8,128)(2,1)S(1)}, u32[]{:S(2)}, u32[]{:S(2)}) collective-permute-start(bf16[2,512,1024]{2,1,0:T(8,128)(2,1)} %get-tuple-element.75), channel_id=1, source_target_pairs={{0,32},{32,0},{1,33},{33,1},{2,34},{34,2},{3,35},{35,3},{4,36},{36... | collective-permute-start | bytes 6291464 | tf_op jit(solution)/shard_map/ppermute | solution.py:523
  100.2 1.4 copy-start.22
  107.1 1.3 copy-start.7
  108.5 7.1 %copy-start.11 = (bf16[512,1024]{1,0:T(8,128)(2,1)}, bf16[512,1024]{1,0:T(8,128)(2,1)S(1)}, u32[]{:S(2)}) copy-start(bf16[512,1024]{1,0:T(8,128)(2,1)S(1)} %get-tuple-element.68) | copy-start | bytes 3145732
  108.5 7.1 %copy-start.13 = (bf16[512,1024]{1,0:T(8,128)(2,1)}, bf16[512,1024]{1,0:T(8,128)(2,1)S(1)}, u32[]{:S(2)}) copy-start(bf16[512,1024]{1,0:T(8,128)(2,1)S(1)} %get-tuple-element.66) | copy-start | bytes 3145732
  108.5 7.9 %copy-start.23 = (bf16[2,512,1024]{2,1,0:T(8,128)(2,1)S(1)}, bf16[2,512,1024]{2,1,0:T(8,128)(2,1)}, u32[]{:S(2)}) copy-start(bf16[2,512,1024]{2,1,0:T(8,128)(2,1)} %get-tuple-element.74) | copy-start | bytes 6291460
  108.5 20.0 %collective-permute-start.5 = (bf16[256,1024]{1,0:T(8,128)(2,1)}, bf16[256,1024]{1,0:T(8,128)(2,1)}, u32[]{:S(2)}, u32[]{:S(2)}) collective-permute-start(bf16[256,1024]{1,0:T(8,128)(2,1)} %get-tuple-element.67), channel_id=1, source_target_pairs={{0,3},{1,2},{2,1},{3,0},{4,7},{5,6},{6,5},{7,4},{8,11},{9,10},{10,... | collective-permute-start | bytes 1572872 | tf_op jit(solution)/shard_map/ppermute | solution.py:560
  115.6 3.1 %copy-start.9 = (bf16[512,512]{1,0:T(8,128)(2,1)}, bf16[512,512]{1,0:T(8,128)(2,1)S(1)}, u32[]{:S(2)}) copy-start(bf16[512,512]{1,0:T(8,128)(2,1)S(1)} %attention_grad.1.grad_t_ref) | copy-start | bytes 1572868
  115.7 15.2 %collective-permute-start.7 = (bf16[256,1024]{1,0:T(8,128)(2,1)}, bf16[256,1024]{1,0:T(8,128)(2,1)S(1)}, u32[]{:S(2)}, u32[]{:S(2)}) collective-permute-start(bf16[256,1024]{1,0:T(8,128)(2,1)} %get-tuple-element.69), channel_id=1, source_target_pairs={{0,1},{1,0},{2,3},{3,2},{4,5},{5,4},{6,7},{7,6},{8,9},{9,8},{10,11... | collective-permute-start | bytes 1572872 | tf_op jit(solution)/shard_map/ppermute | solution.py:560
  118.8 9.8 %copy-start.14 = (bf16[512,1024]{1,0:T(8,128)(2,1)S(1)}, bf16[512,1024]{1,0:T(8,128)(2,1)}, u32[]{:S(2)}) copy-start(bf16[512,1024]{1,0:T(8,128)(2,1)} %copy-done.13) | copy-start | bytes 3145732
  118.8 12.1 %copy-start.12 = (bf16[512,1024]{1,0:T(8,128)(2,1)S(1)}, bf16[512,1024]{1,0:T(8,128)(2,1)}, u32[]{:S(2)}) copy-start(bf16[512,1024]{1,0:T(8,128)(2,1)} %copy-done.11) | copy-start | bytes 3145732
  118.8 43.0 %all-to-all-start.3 = ((bf16[16,64,1024]{2,1,0:T(8,128)(2,1)}), bf16[16,64,1024]{2,1,0:T(8,128)(2,1)}, u32[]{:S(2)}, u32[]{:S(2)}) async-start(bf16[16,64,1024]{2,1,0:T(8,128)(2,1)} %bitcast.42), calls=%async_computation.3 | async-start | bytes 4194304 | tf_op jit(solution)/shard_map/all_to_all | solution.py:518
  128.5 5.1 %copy-start.3 = (bf16[512,512]{1,0:T(8,128)(2,1)S(1)}, bf16[512,512]{1,0:T(8,128)(2,1)}, u32[]{:S(2)}) copy-start(bf16[512,512]{1,0:T(8,128)(2,1)} %copy-done.1) | copy-start | bytes 1572868
  128.5 5.1 %copy-start.10 = (bf16[512,512]{1,0:T(8,128)(2,1)S(1)}, bf16[512,512]{1,0:T(8,128)(2,1)}, u32[]{:S(2)}) copy-start(bf16[512,512]{1,0:T(8,128)(2,1)} %copy-done.9) | copy-start | bytes 1572868
  128.5 5.1 %copy-start.19 = (bf16[512,512]{1,0:T(8,128)(2,1)S(1)}, bf16[512,512]{1,0:T(8,128)(2,1)}, u32[]{:S(2)}) copy-start(bf16[512,512]{1,0:T(8,128)(2,1)} %copy-done.18) | copy-start | bytes 1572868
  128.5 5.1 %copy-start.21 = (f32[4,512]{1,0:T(4,128)S(1)}, f32[4,512]{1,0:T(4,128)}, u32[]{:S(2)}) copy-start(f32[4,512]{1,0:T(4,128)} %copy-done.20) | copy-start | bytes 24580
  129.9 25.1 %collective-permute-start.6 = (bf16[512,1024]{1,0:T(8,128)(2,1)S(1)}, bf16[512,1024]{1,0:T(8,128)(2,1)S(1)}, u32[]{:S(2)}, u32[]{:S(2)}) collective-permute-start(bf16[512,1024]{1,0:T(8,128)(2,1)S(1)} %add_dynamic-update-slice_fusion.1), channel_id=1, source_target_pairs={{0,1},{1,0},{2,3},{3,2},{4,5},{5,4},{6,7},{7,6},{8,9},{9,8},{10,11... | collective-permute-start | bytes 3145736 | tf_op jit(solution)/shard_map/ppermute | solution.py:560
  131.1 26.0 %collective-permute-start.8 = (bf16[512,1024]{1,0:T(8,128)(2,1)S(1)}, bf16[512,1024]{1,0:T(8,128)(2,1)S(1)}, u32[]{:S(2)}, u32[]{:S(2)}) collective-permute-start(bf16[512,1024]{1,0:T(8,128)(2,1)S(1)} %add_dynamic-update-slice_fusion), channel_id=1, source_target_pairs={{0,3},{1,2},{2,1},{3,0},{4,7},{5,6},{6,5},{7,4},{8,11},{9,10},{10,... | collective-permute-start | bytes 3145736 | tf_op jit(solution)/shard_map/ppermute | solution.py:560
  133.6 23.5 %copy-start.8 = (f32[512,1024]{1,0:T(8,128)S(1)}, f32[512,1024]{1,0:T(8,128)}, u32[]{:S(2)}) copy-start(f32[512,1024]{1,0:T(8,128)} %copy-done.7) | copy-start | bytes 6291460
  147.0 11.6 %copy-start.6 = (bf16[4096,256]{1,0:T(8,128)(2,1)}, bf16[4096,256]{1,0:T(8,128)(2,1)S(1)}, u32[]{:S(2)}) copy-start(bf16[4096,256]{1,0:T(8,128)(2,1)S(1)} %get-tuple-element.81) | copy-start | bytes 6291460
  161.8 40.4 %all-to-all-start.2 = ((bf16[32,128,256]{2,1,0:T(8,128)(2,1)}), bf16[32,128,256]{2,1,0:T(8,128)(2,1)S(1)}, u32[]{:S(2)}, u32[]{:S(2)}) async-start(bf16[32,128,256]{2,1,0:T(8,128)(2,1)} %bitcast.40), calls=%async_computation.2 | async-start | bytes 4194304 | tf_op jit(solution)/shard_map/all_to_all | solution.py:518
  167.8 11.1 %collective-permute-start.17 = (f32[64,1024]{1,0:T(8,128)S(1)}, f32[64,1024]{1,0:T(8,128)S(1)}, u32[]{:S(2)}, u32[]{:S(2)}) collective-permute-start(f32[64,1024]{1,0:T(8,128)S(1)} %convert_reduce_fusion), channel_id=1, source_target_pairs={{0,0},{64,1},{32,2},{96,3},{1,32},{65,33},{33,34},{97,35},{2,64},{... | collective-permute-start | bytes 786440 | tf_op jit(solution)/shard_map/ppermute | solution.py:556
  168.6 33.6 %collective-permute-start.14 = (bf16[128,512]{1,0:T(8,128)(2,1)S(1)}, bf16[128,512]{1,0:T(8,128)(2,1)S(1)}, u32[]{:S(2)}, u32[]{:S(2)}) collective-permute-start(bf16[128,512]{1,0:T(8,128)(2,1)S(1)} %get-tuple-element.87), channel_id=1, source_target_pairs={{0,1},{1,2},{2,3},{3,0},{4,5},{5,6},{6,7},{7,4},{8,9},{9,10},{10,1... | collective-permute-start | bytes 393224 | tf_op jit(solution)/shard_map/ppermute | solution.py:523
  171.7 30.5 %collective-permute-start.15 = (bf16[128,512]{1,0:T(8,128)(2,1)S(1)}, bf16[128,512]{1,0:T(8,128)(2,1)S(1)}, u32[]{:S(2)}, u32[]{:S(2)}) collective-permute-start(bf16[128,512]{1,0:T(8,128)(2,1)S(1)} %get-tuple-element.86), channel_id=1, source_target_pairs={{0,2},{1,3},{2,0},{3,1},{4,6},{5,7},{6,4},{7,5},{8,10},{9,11},{10,... | collective-permute-start | bytes 393224 | tf_op jit(solution)/shard_map/ppermute | solution.py:523
  176.4 25.8 %collective-permute-start.16 = (bf16[128,512]{1,0:T(8,128)(2,1)S(1)}, bf16[128,512]{1,0:T(8,128)(2,1)S(1)}, u32[]{:S(2)}, u32[]{:S(2)}) collective-permute-start(bf16[128,512]{1,0:T(8,128)(2,1)S(1)} %get-tuple-element.85), channel_id=1, source_target_pairs={{0,3},{1,0},{2,1},{3,2},{4,7},{5,4},{6,5},{7,6},{8,11},{9,8},{10,9... | collective-permute-start | bytes 393224 | tf_op jit(solution)/shard_map/ppermute | solution.py:523
where the time goes:
time: 205 us; the launch traced here: 204 us
  waiting for transfers between devices  74.4 us (36%)
  starting transfers between devices  60.2 us (29%)
  Pallas kernels  41.8 us (20%)
  local copies, waits for them, and re-layouts  18.8 us (9%)
  other arithmetic  8.21 us (4%)
    ppermute x8, waiting for transfers between devices, shift(): lax.ppermute(array, axis, [(i, (i + by) % length) for i in range(length)])  46.2 us
    all_to_all x4, starting transfers between devices, exchange(): return lax.all_to_all(array, axes, split_axis=0, concat_axis=0, tiled=True)  27.9 us
    ppermute x8, starting transfers between devices, shift(): lax.ppermute(array, axis, [(i, (i + by) % length) for i in range(length)])  16.4 us
    ppermute x8, waiting for transfers between devices, flip(): return lax.ppermute(array, 'x', [(i, i ^ by) for i in range(4)])  14.9 us
    pallas_call x1, Pallas kernels, attend_back(): pl.pallas_call(backward_kernel, name='attention_backward', out_shape=(jax...  13.4 us
    all_to_all x4, waiting for transfers between devices, exchange(): return lax.all_to_all(array, axes, split_axis=0, concat_axis=0, tiled=True)  13.3 us
    ppermute x8, starting transfers between devices, flip(): return lax.ppermute(array, 'x', [(i, i ^ by) for i in range(4)])  13.1 us
    unnamed x49, local copies, waits for them, and re-layouts  11.2 us
  transfers between devices with their start and end apart: 22, of which 11 were waited for; matrix products, arithmetic and copies ran while one was open for 6% of the time, Pallas kernels for 19%

commit v1 on v0

--- a/solution.py
+++ b/solution.py
@@ -17,7 +17,7 @@
 MASKED = -1e30
 BF16 = jnp.bfloat16
 F32 = jnp.float32
-VMEM_LIMIT = 48 * 1024 * 1024
+VMEM_LIMIT = 24 * 1024 * 1024
 SHORT = pl.CostEstimate(flops=1, bytes_accessed=1, transcendentals=0)
 PLANE = ("zhi", "zlo", "y")
 BLOCK = ("zlo", "y")
@@ -310,11 +310,12 @@
     for i, piece in enumerate(pieces):
         columns = pl.ds(pl.multiple_of(target_ref[i] * width, width), width)
         piece[...] = q_ref[0, :, columns]
-        kv_ref[i, :, :HD] = k_ref[0, :, pl.ds(i * HD, HD)]
-        kv_ref[i, :, HD:] = v_ref[0, :, pl.ds(i * HD, HD)]
-
-
-def pack(target, queries, key_vectors, value_vectors):
+        for block in range(kv_ref.shape[0]):
+            kv_ref[block, i, :, :HD] = k_ref[0, :, pl.ds(i * HD, HD)]
+            kv_ref[block, i, :, HD:] = v_ref[0, :, pl.ds(i * HD, HD)]
+
+
+def pack(blocks, target, queries, key_vectors, value_vectors):
     own = queries.shape[1]
     parts = key_vectors.shape[2] // HD
     width = queries.shape[2] // parts
@@ -325,7 +326,7 @@
         name="pack_heads",
         in_specs=[smem, vmem, vmem, vmem],
         out_specs=(vmem,) * (parts + 1),
-        out_shape=(jax.ShapeDtypeStruct((parts, own, 2 * HD), BF16),)
+        out_shape=(jax.ShapeDtypeStruct((blocks, parts, own, 2 * HD), BF16),)
         + (jax.ShapeDtypeStruct((own, width), BF16),) * parts,
     )(target, queries, key_vectors, value_vectors)
 
@@ -587,9 +588,10 @@
     target, source = (x + steps) % xs, (x - steps) % xs
 
     weight_swapped = swap(out_weight)
-    kv_parts, *q_parts = pack(target, queries, key_vectors, value_vectors)
+    kv_parts, *q_parts = pack(blocks, target, queries, key_vectors, value_vectors)
     q_pieces = q_parts[:1] + [shift(q_parts[d], "x", d) for d in range(1, xs)]
-    kv = exchange(spread(kv_parts, blocks), BLOCK + ("x",)).reshape(blocks * rows, 2 * HD)
+    kv_parts = kv_parts.reshape(blocks * xs, own, 2 * HD)
+    kv = exchange(kv_parts, BLOCK + ("x",)).reshape(blocks * rows, 2 * HD)
 
     near = jnp.stack([x, x ^ 1, x ^ 3, x ^ 2]).astype(jnp.int32)
     half = rows // 2

time: 205 us -> 202 us (0.985)
  starting transfers between devices: 60.2 us -> 58 us
    all_to_all x4, waiting for transfers between devices: 13.3 us -> 10.6 us  [exchange(): return lax.all_to_all(array, axes, split_axis=0, concat_axis=0, tiled=True)]
    broadcast_in_dim x2 -> x1, local copies, waits for them, and re-layouts: 5.03 us -> 2.53 us  [spread(): jnp.broadcast_to(array[None], (count,) + array.shape)]
    unnamed x49 -> x55, local copies, waits for them, and re-layouts: 11.2 us -> 11.1 us
  transfers between devices with their start and end apart: 22 -> 22, of which waited for: 11 -> 11; matrix products, arithmetic and copies ran while one was open for 6% -> 7% of each run, Pallas kernels for 19% -> 19%
where the time goes in v1:
time: 202 us
  waiting for transfers between devices  74.9 us (37%)
  starting transfers between devices  58 us (29%)
  Pallas kernels  42.5 us (21%)
  local copies, waits for them, and re-layouts  17.3 us (9%)
  other arithmetic  8.21 us (4%)
    ppermute x8, waiting for transfers between devices, shift(): lax.ppermute(array, axis, [(i, (i + by) % length) for i in range(length)])  47.7 us
    all_to_all x4, starting transfers between devices, exchange(): return lax.all_to_all(array, axes, split_axis=0, concat_axis=0, tiled=True)  28.6 us
    ppermute x8, waiting for transfers between devices, flip(): return lax.ppermute(array, 'x', [(i, i ^ by) for i in range(4)])  16.6 us
    ppermute x8, starting transfers between devices, shift(): lax.ppermute(array, axis, [(i, (i + by) % length) for i in range(length)])  16.2 us
    pallas_call x1, Pallas kernels, attend_back(): pl.pallas_call(backward_kernel, name='attention_backward', out_shape=(jax...  14 us
    ppermute x8, starting transfers between devices, flip(): return lax.ppermute(array, 'x', [(i, i ^ by) for i in range(4)])  11.8 us
    unnamed x55, local copies, waits for them, and re-layouts  11.1 us
    all_to_all x4, waiting for transfers between devices, exchange(): return lax.all_to_all(array, axes, split_axis=0, concat_axis=0, tiled=True)  10.6 us
  transfers between devices with their start and end apart: 22, of which 11 were waited for; matrix products, arithmetic and copies ran while one was open for 7% of the time, Pallas kernels for 19%

profile of v1, /device:TPU:0, one launch (start us, length us, event | category | flops | bytes accessed | tf_op | source)
XLA Modules:
  0.0 201.9 jit_solution(7746128428220890223)
XLA Ops:
  1.2 2.8 %pack_heads.1 = (bf16[8,4,128,256]{3,2,1,0:T(8,128)(2,1)}, bf16[128,512]{1,0:T(8,128)(2,1)}, bf16[128,512]{1,0:T(8,128)(2,1)}, bf16[128,512]{1,0:T(8,128)(2,1)}, bf16[128,512]{1,0:T(8,128)(2,1)}) custom-call(s32[4]{0:T(128)} %and_select_fusion.3.target_ref, bf16[1,128,2048]{2,1,0:T(8,128)(2,1)} %q_ref.1, bf16[1,128,512]{2,1,0:T(8,128)(2,1)} %k_ref.1, ...), custom_call_target="tpu_custom_call" | custom-call | tf_op jit(solution)/shard_map/pack_heads/pallas_call | solution.py:324
  4.0 8.9 %all-to-all-start = ((bf16[32,128,256]{2,1,0:T(8,128)(2,1)}), bf16[32,128,256]{2,1,0:T(8,128)(2,1)S(1)}, u32[]{:S(2)}, u32[]{:S(2)}) async-start(bf16[32,128,256]{2,1,0:T(8,128)(2,1)} %bitcast.46), calls=%async_computation | async-start | bytes 4194304 | tf_op jit(solution)/shard_map/all_to_all | solution.py:519
  12.9 1.9 collective-permute-start.1
  14.8 2.7 %collective-permute-start.2 = (bf16[128,512]{1,0:T(8,128)(2,1)S(1)}, bf16[128,512]{1,0:T(8,128)(2,1)S(1)}, u32[]{:S(2)}, u32[]{:S(2)}) collective-permute-start(bf16[128,512]{1,0:T(8,128)(2,1)S(1)} %copy-done.25), channel_id=1, source_target_pairs={{0,2},{1,3},{2,0},{3,1},{4,6},{5,7},{6,4},{7,5},{8,10},{9,11},{10,... | collective-permute-start | bytes 393224 | tf_op jit(solution)/shard_map/ppermute | solution.py:524
  17.4 1.5 collective-permute-start.3
  19.6 0.8 slice.47
  20.4 21.9 %collective-permute-done.1.refs_1_ = bf16[128,512]{1,0:T(8,128)(2,1)S(1)} collective-permute-done((bf16[128,512]{1,0:T(8,128)(2,1)S(1)}, bf16[128,512]{1,0:T(8,128)(2,1)S(1)}, u32[]{:S(2)}, u32[]{:S(2)}) %collective-permute-start.1) | collective-permute-done | bytes 131104 | tf_op jit(solution)/shard_map/ppermute | solution.py:524
  42.3 2.5 %collective-permute-done.2.refs_2_ = bf16[128,512]{1,0:T(8,128)(2,1)S(1)} collective-permute-done((bf16[128,512]{1,0:T(8,128)(2,1)S(1)}, bf16[128,512]{1,0:T(8,128)(2,1)S(1)}, u32[]{:S(2)}, u32[]{:S(2)}) %collective-permute-start.2) | collective-permute-done | bytes 131104 | tf_op jit(solution)/shard_map/ppermute | solution.py:524
  46.1 4.9 %collective-permute-start.10 = (bf16[1,512,1024]{2,1,0:T(8,128)(2,1)}, bf16[1,512,1024]{2,1,0:T(8,128)(2,1)S(1)}, u32[]{:S(2)}, u32[]{:S(2)}) collective-permute-start(bf16[1,512,1024]{2,1,0:T(8,128)(2,1)} %refs_0_.3), channel_id=1, source_target_pairs={{0,3},{1,2},{2,1},{3,0},{4,7},{5,6},{6,5},{7,4},{8,11},{9,10},{10,... | collective-permute-start | bytes 3145736 | tf_op jit(solution)/shard_map/ppermute | solution.py:561
  51.1 2.5 %broadcast_in_dim.24 = bf16[16,64,1024]{2,1,0:T(8,128)(2,1)} broadcast(bf16[64,1024]{1,0:T(8,128)(2,1)} %copy-done.22), dimensions={1,2} | broadcast | bytes 2228224 | tf_op jit(solution)/shard_map/broadcast_in_dim | solution.py:536
  53.6 5.4 %all-to-all-start.1 = ((bf16[16,64,1024]{2,1,0:T(8,128)(2,1)}), bf16[16,64,1024]{2,1,0:T(8,128)(2,1)S(1)}, u32[]{:S(2)}, u32[]{:S(2)}) async-start(bf16[16,64,1024]{2,1,0:T(8,128)(2,1)} %broadcast_in_dim.24), calls=%async_computation.1 | async-start | bytes 4194304 | tf_op jit(solution)/shard_map/all_to_all | solution.py:519
  59.3 1.6 copy-done.4
  60.9 0.9 copy-done.17
  61.8 9.4 %attention_forward.1 = (bf16[512,512]{1,0:T(8,128)(2,1)S(1)}, bf16[512,512]{1,0:T(8,128)(2,1)S(1)}, f32[4,512]{1,0:T(4,128)S(1)}) custom-call(s32[16]{0:T(128)S(1)} %select_reduce_fusion.order_ref, s32[2]{0:T(128)S(1)} %dynamic_slice.16.rank_ref, s32[4]{0:T(128)S(1)} %and_select_fusion.source_ref, bf16[128,512]{1,0:T(8,128)(2,1)S(1)} %copy-done.15, ...), custom_call_target="tpu_custom_call" | custom-call | flops 4294967296 | bytes 3670016 | tf_op jit(solution)/shard_map/attention_forward/pallas_call | solution.py:159
  71.2 0.8 copy-done
  71.9 0.8 copy-done.18
  73.9 1.6 collective-permute-done.9.refs_1_
  75.5 1.9 slice_bitcast_fusion.1
  77.4 1.4 collective-permute-start.11
  78.8 0.8 slice_bitcast_fusion
  79.6 8.8 %all-to-all-done.1 = bf16[16,64,1024]{2,1,0:T(8,128)(2,1)S(1)} async-done(((bf16[16,64,1024]{2,1,0:T(8,128)(2,1)}), bf16[16,64,1024]{2,1,0:T(8,128)(2,1)S(1)}, u32[]{:S(2)}, u32[]{:S(2)}) %all-to-all-start.1) | async-done | bytes 2097184 | tf_op jit(solution)/shard_map/all_to_all | solution.py:519
  88.5 3.3 %collective-permute-done.11.refs_3_ = bf16[256,1024]{1,0:T(8,128)(2,1)} collective-permute-done((bf16[256,1024]{1,0:T(8,128)(2,1)}, bf16[256,1024]{1,0:T(8,128)(2,1)}, u32[]{:S(2)}, u32[]{:S(2)}) %collective-permute-start.11) | collective-permute-done | bytes 524320 | tf_op jit(solution)/shard_map/ppermute | solution.py:561
  91.8 2.2 %collective-permute-done.12.refs_4_ = bf16[256,1024]{1,0:T(8,128)(2,1)} collective-permute-done((bf16[256,1024]{1,0:T(8,128)(2,1)}, bf16[256,1024]{1,0:T(8,128)(2,1)}, u32[]{:S(2)}, u32[]{:S(2)}) %collective-permute-start.12) | collective-permute-done | bytes 524320 | tf_op jit(solution)/shard_map/ppermute | solution.py:561
  94.0 1.0 copy-done.1
  95.0 4.7 %weight_grad_parts.1 = (bf16[2,512,1024]{2,1,0:T(8,128)(2,1)S(1)}, bf16[2,512,1024]{2,1,0:T(8,128)(2,1)S(1)}) custom-call(s32[4]{0:T(128)S(1)} %pad_add_fusion.group_ref, s32[1]{0:T(128)} %bitcast.4.core_ref, bf16[512,512]{1,0:T(8,128)(2,1)S(1)} %copy-done.1, bf16[1,512,1024]{2,1,0:T(8,128)(2,1)} %refs_0_.3, ...), custom_call_target="tpu_custom_call" | custom-call | flops 1 | bytes 1 | tf_op jit(solution)/shard_map/weight_grad_parts/pallas_call | solution.py:427
  99.8 4.8 %layer_output_parts.1 = (f32[512,1024]{1,0:T(8,128)S(1)}, bf16[512,1024]{1,0:T(8,128)(2,1)S(1)}, bf16[512,1024]{1,0:T(8,128)(2,1)S(1)}, bf16[256,1024]{1,0:T(8,128)(2,1)}, bf16[256,1024]{1,0:T(8,128)(2,1)}) custom-call(s32[4]{0:T(128)S(1)} %pad_add_fusion.group_ref, s32[1]{0:T(128)} %bitcast.4.core_ref, bf16[2,512,1024]{2,1,0:T(8,128)(2,1)S(1)} %bitcast.38, ...), custom_call_target="tpu_custom_call" | custom-call | flops 1 | bytes 1 | tf_op jit(solution)/shard_map/layer_output_parts/pallas_call | solution.py:461
  104.6 1.4 copy-done.7
  106.0 1.0 copy-done.11
  107.0 1.0 copy-done.13
  108.6 5.3 %attention_grad.1.grad_t_ref = bf16[512,512]{1,0:T(8,128)(2,1)S(1)} custom-call(s32[4]{0:T(128)S(1)} %pad_add_fusion.group_ref, s32[1]{0:T(128)} %bitcast.4.core_ref, bf16[2,512,1024]{2,1,0:T(8,128)(2,1)S(1)} %bitcast.39, bf16[2,512,1024]{2,1,0:T(8,128)(2,1)S(1)} %collective-permute-done.4.other_ref, bf16[1,512,1024]{2,1,0:T(8,128)(2,1)} %refs_0_.3, ...), custom_call_target="tpu_custom_call" | custom-call | flops 1 | bytes 1 | tf_op jit(solution)/shard_map/attention_grad/pallas_call | solution.py:389
  113.9 0.8 collective-permute-start.7
  114.7 2.4 %add_convert_fusion = bf16[2,512,1024]{2,1,0:T(8,128)(2,1)} fusion(bf16[2,512,1024]{2,1,0:T(8,128)(2,1)S(1)} %collective-permute-done.13, bf16[2,512,1024]{2,1,0:T(8,128)(2,1)S(1)} %get-tuple-element.74), kind=kLoop, calls=%fused_computation.1 | loop fusion | flops 4194304 | bytes 6291456 | tf_op jit(solution)/shard_map/convert_element_type | solution.py:617
  117.1 8.4 %all-to-all-start.3 = ((bf16[16,64,1024]{2,1,0:T(8,128)(2,1)}), bf16[16,64,1024]{2,1,0:T(8,128)(2,1)}, u32[]{:S(2)}, u32[]{:S(2)}) async-start(bf16[16,64,1024]{2,1,0:T(8,128)(2,1)} %bitcast.45), calls=%async_computation.3 | async-start | bytes 4194304 | tf_op jit(solution)/shard_map/all_to_all | solution.py:519
  125.6 1.4 add_dynamic-update-slice_fusion.1
  127.0 1.4 collective-permute-start.6
  128.6 2.6 %collective-permute-start.8 = (bf16[512,1024]{1,0:T(8,128)(2,1)S(1)}, bf16[512,1024]{1,0:T(8,128)(2,1)S(1)}, u32[]{:S(2)}, u32[]{:S(2)}) collective-permute-start(bf16[512,1024]{1,0:T(8,128)(2,1)S(1)} %add_dynamic-update-slice_fusion), channel_id=1, source_target_pairs={{0,3},{1,2},{2,1},{3,0},{4,7},{5,6},{6,5},{7,4},{8,11},{9,10},{10,... | collective-permute-start | bytes 3145736 | tf_op jit(solution)/shard_map/ppermute | solution.py:561
  131.2 14.0 %attention_backward.1 = (bf16[512,512]{1,0:T(8,128)(2,1)S(1)}, bf16[4096,256]{1,0:T(8,128)(2,1)S(1)}) custom-call(s32[2]{0:T(128)S(1)} %dynamic_slice.16.rank_ref, s32[16]{0:T(128)S(1)} %and_select_fusion.1.key_rank_ref, bf16[512,512]{1,0:T(8,128)(2,1)S(1)} %copy-done.19, bf16[4096,256]{1,0:T(8,128)(2,1)S(1)} %bitcast.42, bf16[512,512]{1,0:T(8,128)(2,1)S(1)} %copy-done.10, ...), custom_call_target="tpu_custom_call" | custom-call | flops 10737418240 | bytes 6291456 | tf_op jit(solution)/shard_map/attention_backward/pallas_call | solution.py:282
  145.3 6.5 %collective-permute-done.6 = bf16[512,1024]{1,0:T(8,128)(2,1)S(1)} collective-permute-done((bf16[512,1024]{1,0:T(8,128)(2,1)S(1)}, bf16[512,1024]{1,0:T(8,128)(2,1)S(1)}, u32[]{:S(2)}, u32[]{:S(2)}) %collective-permute-start.6) | collective-permute-done | bytes 1048608 | tf_op jit(solution)/shard_map/ppermute | solution.py:561
  151.8 2.5 %collective-permute-done.8 = bf16[512,1024]{1,0:T(8,128)(2,1)S(1)} collective-permute-done((bf16[512,1024]{1,0:T(8,128)(2,1)S(1)}, bf16[512,1024]{1,0:T(8,128)(2,1)S(1)}, u32[]{:S(2)}, u32[]{:S(2)}) %collective-permute-start.8) | collective-permute-done | bytes 1048608 | tf_op jit(solution)/shard_map/ppermute | solution.py:561
  154.3 1.5 fusion
  155.8 1.8 all-to-all-done.3
  157.5 5.9 %all-to-all-start.2 = ((bf16[32,128,256]{2,1,0:T(8,128)(2,1)}), bf16[32,128,256]{2,1,0:T(8,128)(2,1)S(1)}, u32[]{:S(2)}, u32[]{:S(2)}) async-start(bf16[32,128,256]{2,1,0:T(8,128)(2,1)} %bitcast.43), calls=%async_computation.2 | async-start | bytes 4194304 | tf_op jit(solution)/shard_map/all_to_all | solution.py:519
  163.4 2.0 convert_reduce_fusion
  166.2 3.1 %collective-permute-start.14 = (bf16[128,512]{1,0:T(8,128)(2,1)S(1)}, bf16[128,512]{1,0:T(8,128)(2,1)S(1)}, u32[]{:S(2)}, u32[]{:S(2)}) collective-permute-start(bf16[128,512]{1,0:T(8,128)(2,1)S(1)} %get-tuple-element.87), channel_id=1, source_target_pairs={{0,1},{1,2},{2,3},{3,0},{4,5},{5,6},{6,7},{7,4},{8,9},{9,10},{10,1... | collective-permute-start | bytes 393224 | tf_op jit(solution)/shard_map/ppermute | solution.py:524
  169.3 4.5 %collective-permute-start.15 = (bf16[128,512]{1,0:T(8,128)(2,1)S(1)}, bf16[128,512]{1,0:T(8,128)(2,1)S(1)}, u32[]{:S(2)}, u32[]{:S(2)}) collective-permute-start(bf16[128,512]{1,0:T(8,128)(2,1)S(1)} %get-tuple-element.86), channel_id=1, source_target_pairs={{0,2},{1,3},{2,0},{3,1},{4,6},{5,7},{6,4},{7,5},{8,10},{9,11},{10,... | collective-permute-start | bytes 393224 | tf_op jit(solution)/shard_map/ppermute | solution.py:524
  173.9 2.5 %collective-permute-start.16 = (bf16[128,512]{1,0:T(8,128)(2,1)S(1)}, bf16[128,512]{1,0:T(8,128)(2,1)S(1)}, u32[]{:S(2)}, u32[]{:S(2)}) collective-permute-start(bf16[128,512]{1,0:T(8,128)(2,1)S(1)} %get-tuple-element.85), channel_id=1, source_target_pairs={{0,3},{1,0},{2,1},{3,2},{4,7},{5,4},{6,5},{7,6},{8,11},{9,8},{10,9... | collective-permute-start | bytes 393224 | tf_op jit(solution)/shard_map/ppermute | solution.py:524
  176.4 23.2 %collective-permute-done.14.refs_1_ = bf16[128,512]{1,0:T(8,128)(2,1)S(1)} collective-permute-done((bf16[128,512]{1,0:T(8,128)(2,1)S(1)}, bf16[128,512]{1,0:T(8,128)(2,1)S(1)}, u32[]{:S(2)}, u32[]{:S(2)}) %collective-permute-start.14) | collective-permute-done | bytes 131104 | tf_op jit(solution)/shard_map/ppermute | solution.py:524
  199.6 1.6 gather_gradients.1
  (75 shorter events, 6.4 us)
Async XLA Ops:
  4.0 8.9 %copy-start.26 = (bf16[128,512]{1,0:T(8,128)(2,1)S(1)}, bf16[128,512]{1,0:T(8,128)(2,1)}, u32[]{:S(2)}) copy-start(bf16[128,512]{1,0:T(8,128)(2,1)} %get-tuple-element.59) | copy-start | bytes 393220
  4.0 10.8 %copy-start.25 = (bf16[128,512]{1,0:T(8,128)(2,1)S(1)}, bf16[128,512]{1,0:T(8,128)(2,1)}, u32[]{:S(2)}) copy-start(bf16[128,512]{1,0:T(8,128)(2,1)} %get-tuple-element.60) | copy-start | bytes 393220
  4.0 13.5 %copy-start.24 = (bf16[128,512]{1,0:T(8,128)(2,1)S(1)}, bf16[128,512]{1,0:T(8,128)(2,1)}, u32[]{:S(2)}) copy-start(bf16[128,512]{1,0:T(8,128)(2,1)} %get-tuple-element.61) | copy-start | bytes 393220
  4.0 14.9 %copy-start.23 = (bf16[64,1024]{1,0:T(8,128)(2,1)S(1)}, bf16[64,1024]{1,0:T(8,128)(2,1)}, u32[]{:S(2)}) copy-start(bf16[64,1024]{1,0:T(8,128)(2,1)} %param.14) | copy-start | bytes 393220
  4.0 41.5 %all-to-all-start = ((bf16[32,128,256]{2,1,0:T(8,128)(2,1)}), bf16[32,128,256]{2,1,0:T(8,128)(2,1)S(1)}, u32[]{:S(2)}, u32[]{:S(2)}) async-start(bf16[32,128,256]{2,1,0:T(8,128)(2,1)} %bitcast.46), calls=%async_computation | async-start | bytes 4194304 | tf_op jit(solution)/shard_map/all_to_all | solution.py:519
  12.9 29.4 %collective-permute-start.1 = (bf16[128,512]{1,0:T(8,128)(2,1)S(1)}, bf16[128,512]{1,0:T(8,128)(2,1)S(1)}, u32[]{:S(2)}, u32[]{:S(2)}) collective-permute-start(bf16[128,512]{1,0:T(8,128)(2,1)S(1)} %copy-done.26), channel_id=1, source_target_pairs={{0,1},{1,2},{2,3},{3,0},{4,5},{5,6},{6,7},{7,4},{8,9},{9,10},{10,1... | collective-permute-start | bytes 393224 | tf_op jit(solution)/shard_map/ppermute | solution.py:524
  14.8 30.1 %collective-permute-start.2 = (bf16[128,512]{1,0:T(8,128)(2,1)S(1)}, bf16[128,512]{1,0:T(8,128)(2,1)S(1)}, u32[]{:S(2)}, u32[]{:S(2)}) collective-permute-start(bf16[128,512]{1,0:T(8,128)(2,1)S(1)} %copy-done.25), channel_id=1, source_target_pairs={{0,2},{1,3},{2,0},{3,1},{4,6},{5,7},{6,4},{7,5},{8,10},{9,11},{10,... | collective-permute-start | bytes 393224 | tf_op jit(solution)/shard_map/ppermute | solution.py:524
  17.4 27.4 %collective-permute-start.3 = (bf16[128,512]{1,0:T(8,128)(2,1)S(1)}, bf16[128,512]{1,0:T(8,128)(2,1)S(1)}, u32[]{:S(2)}, u32[]{:S(2)}) collective-permute-start(bf16[128,512]{1,0:T(8,128)(2,1)S(1)} %copy-done.24), channel_id=1, source_target_pairs={{0,3},{1,0},{2,1},{3,2},{4,7},{5,4},{6,5},{7,6},{8,11},{9,8},{10,9... | collective-permute-start | bytes 393224 | tf_op jit(solution)/shard_map/ppermute | solution.py:524
  18.9 26.6 %collective-permute-start = (bf16[64,1024]{1,0:T(8,128)(2,1)S(1)}, bf16[64,1024]{1,0:T(8,128)(2,1)S(1)}, u32[]{:S(2)}, u32[]{:S(2)}) collective-permute-start(bf16[64,1024]{1,0:T(8,128)(2,1)S(1)} %copy-done.23), channel_id=1, source_target_pairs={{0,0},{1,64},{2,32},{3,96},{32,1},{33,65},{34,33},{35,97},{64,2},{... | collective-permute-start | bytes 393224 | tf_op jit(solution)/shard_map/ppermute | solution.py:553
  44.8 0.7 copy-start.16
  45.5 0.7 copy-start.22
  45.5 8.1 %copy-start.3 = (bf16[32,128,256]{2,1,0:T(8,128)(2,1)}, bf16[32,128,256]{2,1,0:T(8,128)(2,1)S(1)}, u32[]{:S(2)}) copy-start(bf16[32,128,256]{2,1,0:T(8,128)(2,1)S(1)} %all-to-all-done) | copy-start | bytes 6291460
  46.1 27.8 %collective-permute-start.10 = (bf16[1,512,1024]{2,1,0:T(8,128)(2,1)}, bf16[1,512,1024]{2,1,0:T(8,128)(2,1)S(1)}, u32[]{:S(2)}, u32[]{:S(2)}) collective-permute-start(bf16[1,512,1024]{2,1,0:T(8,128)(2,1)} %refs_0_.3), channel_id=1, source_target_pairs={{0,3},{1,2},{2,1},{3,0},{4,7},{5,6},{6,5},{7,4},{8,11},{9,10},{10,... | collective-permute-start | bytes 3145736 | tf_op jit(solution)/shard_map/ppermute | solution.py:561
  51.1 24.4 %collective-permute-start.9 = (bf16[1,512,1024]{2,1,0:T(8,128)(2,1)}, bf16[1,512,1024]{2,1,0:T(8,128)(2,1)}, u32[]{:S(2)}, u32[]{:S(2)}) collective-permute-start(bf16[1,512,1024]{2,1,0:T(8,128)(2,1)} %refs_0_.3), channel_id=1, source_target_pairs={{0,1},{1,0},{2,3},{3,2},{4,5},{5,4},{6,7},{7,6},{8,9},{9,8},{10,11... | collective-permute-start | bytes 3145736 | tf_op jit(solution)/shard_map/ppermute | solution.py:561
  53.6 5.6 %copy-start.15 = (bf16[128,512]{1,0:T(8,128)(2,1)S(1)}, bf16[128,512]{1,0:T(8,128)(2,1)}, u32[]{:S(2)}) copy-start(bf16[128,512]{1,0:T(8,128)(2,1)} %get-tuple-element.58.refs_0_) | copy-start | bytes 393220
  53.6 34.8 %all-to-all-start.1 = ((bf16[16,64,1024]{2,1,0:T(8,128)(2,1)}), bf16[16,64,1024]{2,1,0:T(8,128)(2,1)S(1)}, u32[]{:S(2)}, u32[]{:S(2)}) async-start(bf16[16,64,1024]{2,1,0:T(8,128)(2,1)} %broadcast_in_dim.24), calls=%async_computation.1 | async-start | bytes 4194304 | tf_op jit(solution)/shard_map/all_to_all | solution.py:519
  59.3 1.6 copy-start.4
  60.9 0.9 copy-start.17
  71.2 0.8 copy-start
  71.9 0.8 copy-start.18
  77.4 14.4 %collective-permute-start.11 = (bf16[256,1024]{1,0:T(8,128)(2,1)}, bf16[256,1024]{1,0:T(8,128)(2,1)}, u32[]{:S(2)}, u32[]{:S(2)}) collective-permute-start(bf16[256,1024]{1,0:T(8,128)(2,1)} %slice_bitcast_fusion.1), channel_id=1, source_target_pairs={{0,3},{1,2},{2,1},{3,0},{4,7},{5,6},{6,5},{7,4},{8,11},{9,10},{10,... | collective-permute-start | bytes 1572872 | tf_op jit(solution)/shard_map/ppermute | solution.py:561
  79.6 14.4 %collective-permute-start.12 = (bf16[256,1024]{1,0:T(8,128)(2,1)}, bf16[256,1024]{1,0:T(8,128)(2,1)}, u32[]{:S(2)}, u32[]{:S(2)}) collective-permute-start(bf16[256,1024]{1,0:T(8,128)(2,1)} %slice_bitcast_fusion), channel_id=1, source_target_pairs={{0,1},{1,0},{2,3},{3,2},{4,5},{5,4},{6,7},{7,6},{8,9},{9,8},{10,11... | collective-permute-start | bytes 1572872 | tf_op jit(solution)/shard_map/ppermute | solution.py:561
  88.4 11.4 %collective-permute-start.4 = (bf16[2,512,1024]{2,1,0:T(8,128)(2,1)S(1)}, bf16[2,512,1024]{2,1,0:T(8,128)(2,1)S(1)}, u32[]{:S(2)}, u32[]{:S(2)}) collective-permute-start(bf16[2,512,1024]{2,1,0:T(8,128)(2,1)S(1)} %bitcast.37), channel_id=1, source_target_pairs={{0,32},{32,0},{1,33},{33,1},{2,34},{34,2},{3,35},{35,3},{4,36},{36... | collective-permute-start | bytes 6291464 | tf_op jit(solution)/shard_map/ppermute | solution.py:524
  94.0 1.0 copy-start.1
  99.7 14.1 %collective-permute-start.13 = (bf16[2,512,1024]{2,1,0:T(8,128)(2,1)S(1)}, bf16[2,512,1024]{2,1,0:T(8,128)(2,1)S(1)}, u32[]{:S(2)}, u32[]{:S(2)}) collective-permute-start(bf16[2,512,1024]{2,1,0:T(8,128)(2,1)S(1)} %get-tuple-element.75), channel_id=1, source_target_pairs={{0,32},{32,0},{1,33},{33,1},{2,34},{34,2},{3,35},{35,3},{4,36},{36... | collective-permute-start | bytes 6291464 | tf_op jit(solution)/shard_map/ppermute | solution.py:524
  104.6 1.4 copy-start.7
  106.0 1.0 copy-start.11
  107.0 1.0 copy-start.13
  107.9 17.6 %collective-permute-start.5 = (bf16[256,1024]{1,0:T(8,128)(2,1)}, bf16[256,1024]{1,0:T(8,128)(2,1)}, u32[]{:S(2)}, u32[]{:S(2)}) collective-permute-start(bf16[256,1024]{1,0:T(8,128)(2,1)} %get-tuple-element.67), channel_id=1, source_target_pairs={{0,3},{1,2},{2,1},{3,0},{4,7},{5,6},{6,5},{7,4},{8,11},{9,10},{10,... | collective-permute-start | bytes 1572872 | tf_op jit(solution)/shard_map/ppermute | solution.py:561
  113.8 3.2 %copy-start.9 = (bf16[512,512]{1,0:T(8,128)(2,1)}, bf16[512,512]{1,0:T(8,128)(2,1)S(1)}, u32[]{:S(2)}) copy-start(bf16[512,512]{1,0:T(8,128)(2,1)S(1)} %attention_grad.1.grad_t_ref) | copy-start | bytes 1572868
  113.9 14.5 %collective-permute-start.7 = (bf16[256,1024]{1,0:T(8,128)(2,1)}, bf16[256,1024]{1,0:T(8,128)(2,1)S(1)}, u32[]{:S(2)}, u32[]{:S(2)}) collective-permute-start(bf16[256,1024]{1,0:T(8,128)(2,1)} %get-tuple-element.69), channel_id=1, source_target_pairs={{0,1},{1,0},{2,3},{3,2},{4,5},{5,4},{6,7},{7,6},{8,9},{9,8},{10,11... | collective-permute-start | bytes 1572872 | tf_op jit(solution)/shard_map/ppermute | solution.py:561
  117.1 8.5 %copy-start.14 = (bf16[512,1024]{1,0:T(8,128)(2,1)S(1)}, bf16[512,1024]{1,0:T(8,128)(2,1)}, u32[]{:S(2)}) copy-start(bf16[512,1024]{1,0:T(8,128)(2,1)} %copy-done.13) | copy-start | bytes 3145732
  117.1 11.3 %copy-start.12 = (bf16[512,1024]{1,0:T(8,128)(2,1)S(1)}, bf16[512,1024]{1,0:T(8,128)(2,1)}, u32[]{:S(2)}) copy-start(bf16[512,1024]{1,0:T(8,128)(2,1)} %copy-done.11) | copy-start | bytes 3145732
  117.1 14.1 %copy-start.19 = (bf16[512,512]{1,0:T(8,128)(2,1)S(1)}, bf16[512,512]{1,0:T(8,128)(2,1)}, u32[]{:S(2)}) copy-start(bf16[512,512]{1,0:T(8,128)(2,1)} %copy-done.18) | copy-start | bytes 1572868
  117.1 14.1 %copy-start.21 = (f32[4,512]{1,0:T(4,128)S(1)}, f32[4,512]{1,0:T(4,128)}, u32[]{:S(2)}) copy-start(f32[4,512]{1,0:T(4,128)} %copy-done.20) | copy-start | bytes 24580
  117.1 40.4 %all-to-all-start.3 = ((bf16[16,64,1024]{2,1,0:T(8,128)(2,1)}), bf16[16,64,1024]{2,1,0:T(8,128)(2,1)}, u32[]{:S(2)}, u32[]{:S(2)}) async-start(bf16[16,64,1024]{2,1,0:T(8,128)(2,1)} %bitcast.45), calls=%async_computation.3 | async-start | bytes 4194304 | tf_op jit(solution)/shard_map/all_to_all | solution.py:519
  125.5 5.7 %copy-start.2 = (bf16[512,512]{1,0:T(8,128)(2,1)S(1)}, bf16[512,512]{1,0:T(8,128)(2,1)}, u32[]{:S(2)}) copy-start(bf16[512,512]{1,0:T(8,128)(2,1)} %copy-done) | copy-start | bytes 1572868
  125.5 5.7 %copy-start.5 = (bf16[32,128,256]{2,1,0:T(8,128)(2,1)S(1)}, bf16[32,128,256]{2,1,0:T(8,128)(2,1)}, u32[]{:S(2)}) copy-start(bf16[32,128,256]{2,1,0:T(8,128)(2,1)} %copy-done.3) | copy-start | bytes 6291460
  125.5 5.7 %copy-start.10 = (bf16[512,512]{1,0:T(8,128)(2,1)S(1)}, bf16[512,512]{1,0:T(8,128)(2,1)}, u32[]{:S(2)}) copy-start(bf16[512,512]{1,0:T(8,128)(2,1)} %copy-done.9) | copy-start | bytes 1572868
  127.0 24.8 %collective-permute-start.6 = (bf16[512,1024]{1,0:T(8,128)(2,1)S(1)}, bf16[512,1024]{1,0:T(8,128)(2,1)S(1)}, u32[]{:S(2)}, u32[]{:S(2)}) collective-permute-start(bf16[512,1024]{1,0:T(8,128)(2,1)S(1)} %add_dynamic-update-slice_fusion.1), channel_id=1, source_target_pairs={{0,1},{1,0},{2,3},{3,2},{4,5},{5,4},{6,7},{7,6},{8,9},{9,8},{10,11... | collective-permute-start | bytes 3145736 | tf_op jit(solution)/shard_map/ppermute | solution.py:561
  128.6 25.7 %collective-permute-start.8 = (bf16[512,1024]{1,0:T(8,128)(2,1)S(1)}, bf16[512,1024]{1,0:T(8,128)(2,1)S(1)}, u32[]{:S(2)}, u32[]{:S(2)}) collective-permute-start(bf16[512,1024]{1,0:T(8,128)(2,1)S(1)} %add_dynamic-update-slice_fusion), channel_id=1, source_target_pairs={{0,3},{1,2},{2,1},{3,0},{4,7},{5,6},{6,5},{7,4},{8,11},{9,10},{10,... | collective-permute-start | bytes 3145736 | tf_op jit(solution)/shard_map/ppermute | solution.py:561
  131.2 23.0 %copy-start.8 = (f32[512,1024]{1,0:T(8,128)S(1)}, f32[512,1024]{1,0:T(8,128)}, u32[]{:S(2)}) copy-start(f32[512,1024]{1,0:T(8,128)} %copy-done.7) | copy-start | bytes 6291460
  145.3 10.5 %copy-start.6 = (bf16[4096,256]{1,0:T(8,128)(2,1)}, bf16[4096,256]{1,0:T(8,128)(2,1)S(1)}, u32[]{:S(2)}) copy-start(bf16[4096,256]{1,0:T(8,128)(2,1)S(1)} %get-tuple-element.81) | copy-start | bytes 6291460
  157.5 42.1 %all-to-all-start.2 = ((bf16[32,128,256]{2,1,0:T(8,128)(2,1)}), bf16[32,128,256]{2,1,0:T(8,128)(2,1)S(1)}, u32[]{:S(2)}, u32[]{:S(2)}) async-start(bf16[32,128,256]{2,1,0:T(8,128)(2,1)} %bitcast.43), calls=%async_computation.2 | async-start | bytes 4194304 | tf_op jit(solution)/shard_map/all_to_all | solution.py:519
  165.5 10.9 %collective-permute-start.17 = (f32[64,1024]{1,0:T(8,128)S(1)}, f32[64,1024]{1,0:T(8,128)S(1)}, u32[]{:S(2)}, u32[]{:S(2)}) collective-permute-start(f32[64,1024]{1,0:T(8,128)S(1)} %convert_reduce_fusion), channel_id=1, source_target_pairs={{0,0},{64,1},{32,2},{96,3},{1,32},{65,33},{33,34},{97,35},{2,64},{... | collective-permute-start | bytes 786440 | tf_op jit(solution)/shard_map/ppermute | solution.py:557
  166.2 33.4 %collective-permute-start.14 = (bf16[128,512]{1,0:T(8,128)(2,1)S(1)}, bf16[128,512]{1,0:T(8,128)(2,1)S(1)}, u32[]{:S(2)}, u32[]{:S(2)}) collective-permute-start(bf16[128,512]{1,0:T(8,128)(2,1)S(1)} %get-tuple-element.87), channel_id=1, source_target_pairs={{0,1},{1,2},{2,3},{3,0},{4,5},{5,6},{6,7},{7,4},{8,9},{9,10},{10,1... | collective-permute-start | bytes 393224 | tf_op jit(solution)/shard_map/ppermute | solution.py:524
  169.3 30.3 %collective-permute-start.15 = (bf16[128,512]{1,0:T(8,128)(2,1)S(1)}, bf16[128,512]{1,0:T(8,128)(2,1)S(1)}, u32[]{:S(2)}, u32[]{:S(2)}) collective-permute-start(bf16[128,512]{1,0:T(8,128)(2,1)S(1)} %get-tuple-element.86), channel_id=1, source_target_pairs={{0,2},{1,3},{2,0},{3,1},{4,6},{5,7},{6,4},{7,5},{8,10},{9,11},{10,... | collective-permute-start | bytes 393224 | tf_op jit(solution)/shard_map/ppermute | solution.py:524
  173.9 25.8 %collective-permute-start.16 = (bf16[128,512]{1,0:T(8,128)(2,1)S(1)}, bf16[128,512]{1,0:T(8,128)(2,1)S(1)}, u32[]{:S(2)}, u32[]{:S(2)}) collective-permute-start(bf16[128,512]{1,0:T(8,128)(2,1)S(1)} %get-tuple-element.85), channel_id=1, source_target_pairs={{0,3},{1,0},{2,1},{3,2},{4,7},{5,4},{6,5},{7,6},{8,11},{9,8},{10,9... | collective-permute-start | bytes 393224 | tf_op jit(solution)/shard_map/ppermute | solution.py:524
  (1 other events, 0.6 us)
